TPU v7x, 32 devices: a whole 2x2x4 slice. The times are simulated.
32 devices in a mesh: dp: 8 (over z, y), mp: 4 (over x, core).
Axes of the slice: x: 2, y: 2, z: 4, core: 2. Of those that a mesh axis runs over, the one named last changes fastest.
Arguments:
- hidden: bfloat16 [64, 32, 1024], P(('dp', 'mp')), may hold values from -96 to 96, as said below
- query_weight: bfloat16 [1024, 1024], P('dp', 'mp'), may hold values from -0.1875 to 0.1875
- w_key: bfloat16 [1024, 1024], P('dp', 'mp'), may hold values from -0.1875 to 0.1875
- w_value: bfloat16 [1024, 1024], P('dp', 'mp'), may hold values from -0.1875 to 0.1875
- rel_table: bfloat16 [512, 1024], P('dp'), may hold values from -6 to 6
- rel_bucket: int32 [32, 32], replicated, may hold values from 0 to 511
- w_out: bfloat16 [1024, 1024], P('mp', 'dp'), may hold values from -0.1875 to 0.1875
- w_up: bfloat16 [1024, 4096], P('dp', 'mp'), may hold values from -0.1875 to 0.1875
- w_down: bfloat16 [4096, 1024], P('mp', 'dp'), may hold values from -0.09375 to 0.09375
- w_proj: bfloat16 [1024, 128], P(('dp', 'mp')), may hold values from -0.1875 to 0.1875
- pages: bfloat16 [2048, 128, 128], P('dp'), may hold values from -0.59765625 to 0.59765625
- page_len: int32 [2048], P('dp'), may hold values from 1 to 128
- slot_per_page: int32 [2048], replicated, may hold values from 0 to 2047, as said below
- candidates: int32 [64, 16, 4], P(('dp', 'mp')), may hold values from 0 to 2047, as said below
Outputs:
- query_vectors: bfloat16 [64, 32, 128], P(('dp', 'mp'))
- scores: float32 [64, 16], P(('dp', 'mp'))
Inputs may be any that keep to these rules, and one draw needn't show every extreme that they name: slot_per_page is a permutation of the slots; the page in slot s is held by index s // 256 of dp. `candidates`: among the 128 page ids of the 2 queries of one device (queries in aligned blocks of 2), at most 32 have slots held by any one index of dp, and in every such block some index of dp holds exactly 32 of them. `hidden`: token states are finite.
All inputs are finite; a program needn't handle non-finite values.
Results may differ from a plain program's by a relative error of at most 0.025.
Values may be sent and summed in bfloat16 or wider, within the bound.
A program may use at most 64 MiB of HBM per device.

v0:
```python
import jax
import jax.numpy as jnp
from jax import lax
from jax.sharding import PartitionSpec as P

HD = 64


def layer_norm(value):
    mean = jnp.mean(value, axis=-1, keepdims=True)
    centered = value - mean
    var = jnp.mean(centered * centered, axis=-1, keepdims=True)
    return centered / jnp.sqrt(var + 1e-07)


def add_rows(left, piece):
    return jnp.dot(left, piece, preferred_element_type=jnp.float32)


def return_maxima(maxima):
    return lax.all_to_all(
        maxima.astype(jnp.bfloat16), "dp", split_axis=0, concat_axis=0, tiled=True
    ).astype(maxima.dtype)


def body(
    hidden,
    query_weight,
    w_key,
    w_value,
    rel_table,
    rel_bucket,
    w_out,
    w_up,
    w_down,
    w_proj,
    pages,
    page_len,
    slot_per_page,
    candidates,
):
    qry_dev, qlen, width = hidden.shape
    heads_local = query_weight.shape[1] // HD
    cols = query_weight.shape[1]
    tokens = lax.all_gather(hidden, "mp", axis=0, tiled=True)
    group = tokens.shape[0]
    flat = tokens.reshape(group * qlen, width)
    left_rel = lax.all_gather(rel_table, "dp", axis=0, tiled=True)
    pieces = (
        lax.all_gather(query_weight, "dp", axis=0, tiled=True),
        lax.all_gather(w_key, "dp", axis=0, tiled=True),
        lax.all_gather(w_value, "dp", axis=0, tiled=True),
    )
    qsum = add_rows(flat, pieces[0])
    ksum = add_rows(flat, pieces[1])
    vsum = add_rows(flat, pieces[2])
    qrsum = add_rows(left_rel, pieces[0])
    krsum = add_rows(left_rel, pieces[1])
    rel_q = qrsum.astype(jnp.bfloat16)
    rel_k = krsum.astype(jnp.bfloat16)
    nbuck = rel_q.shape[0]
    qx = qsum.astype(jnp.bfloat16).reshape(group, qlen, heads_local, HD)
    kx = ksum.astype(jnp.bfloat16).reshape(group, qlen, heads_local, HD)
    vx = vsum.astype(jnp.bfloat16).reshape(group, qlen, heads_local, HD)
    rel_q = rel_q.reshape(nbuck, heads_local, HD)
    rel_k = rel_k.reshape(nbuck, heads_local, HD)
    onehot = (rel_bucket[:, :, None] == jnp.arange(nbuck, dtype=jnp.int32)[None, None, :]).astype(
        jnp.float32
    )
    scale = 1.0 / jnp.sqrt(jnp.float32(3 * HD))
    content = jnp.einsum("qihd,qjhd->qhij", qx, kx, preferred_element_type=jnp.float32)
    along_axis_name = jnp.einsum("qihd,bhd->qhib", qx, rel_k, preferred_element_type=jnp.float32)
    c2p = jnp.einsum("qhib,ijb->qhij", along_axis_name, onehot, precision=lax.Precision.HIGHEST)
    back = jnp.einsum("qjhd,bhd->qhjb", kx, rel_q, preferred_element_type=jnp.float32)
    p2c = jnp.einsum("qhjb,jib->qhij", back, onehot, precision=lax.Precision.HIGHEST)
    logits = (content + c2p + p2c) * scale
    probs = jax.nn.softmax(logits, axis=-1).astype(jnp.bfloat16)
    context_rows = jnp.einsum("qhij,qjhd->qihd", probs, vx, preferred_element_type=jnp.float32)
    context_rows = context_rows.astype(jnp.bfloat16).reshape(group * qlen, cols)
    attn_terms = jnp.dot(
        context_rows,
        lax.all_gather(w_out, "dp", axis=1, tiled=True),
        preferred_element_type=jnp.float32,
    )
    attn = lax.psum_scatter(
        attn_terms.astype(jnp.bfloat16), "mp", scatter_dimension=0, tiled=True
    ).astype(jnp.float32)
    own = hidden.reshape(qry_dev * qlen, width).astype(jnp.float32)
    mid = layer_norm(own + attn).astype(jnp.bfloat16)
    mid_all = lax.all_gather(mid, "mp", axis=0, tiled=True)
    up = add_rows(mid_all, lax.all_gather(w_up, "dp", axis=0, tiled=True))
    inner = jax.nn.gelu(up, approximate=False).astype(jnp.bfloat16)
    down_terms = jnp.dot(
        inner, lax.all_gather(w_down, "dp", axis=1, tiled=True), preferred_element_type=jnp.float32
    )
    mlp = lax.psum_scatter(
        down_terms.astype(jnp.bfloat16), "mp", scatter_dimension=0, tiled=True
    ).astype(jnp.float32)
    state = layer_norm(mid.astype(jnp.float32) + mlp).astype(jnp.bfloat16)
    width_out = w_proj.shape[1]
    proj = add_rows(state, lax.all_gather(w_proj, ("dp", "mp"), axis=0, tiled=True))
    vectors = (proj / jnp.sqrt(jnp.sum(proj * proj, axis=-1, keepdims=True) + 1e-06)).astype(
        jnp.bfloat16
    )
    vectors = vectors.reshape(qry_dev, qlen, width_out)
    page_owners = lax.axis_size("dp")
    pg_dev = pages.shape[0]
    ptok = pages.shape[1]
    ncand, ppc = (candidates.shape[1], candidates.shape[2])
    req = qry_dev * ncand * ppc
    cap = 2 * req // page_owners
    slots = slot_per_page[candidates.reshape(req)]
    dest = slots // pg_dev
    local = slots % pg_dev
    query_of = jnp.arange(req, dtype=jnp.int32) // (ncand * ppc)
    member = (dest[:, None] == jnp.arange(page_owners, dtype=jnp.int32)[None, :]).astype(jnp.int32)
    place = jnp.sum((jnp.cumsum(member, axis=0) - 1) * member, axis=1)
    index = dest * cap + place
    codes = jnp.full((page_owners * cap,), -1, jnp.int32).at[index].set(query_of * pg_dev + local)
    codes = codes.reshape(page_owners, cap)
    token_positions = jnp.arange(ptok, dtype=jnp.int32)
    rows_out = (
        jnp.zeros((page_owners * cap, qlen, width_out), jnp.bfloat16)
        .at[index]
        .set(vectors[query_of])
    )
    rows_out = rows_out.reshape(page_owners, cap, qlen, width_out)
    where_local = lax.all_to_all(codes, "dp", split_axis=0, concat_axis=0, tiled=True) % pg_dev
    chosen = pages[where_local]
    lens = page_len[where_local]
    sim = jnp.einsum(
        "snie,snte->snit",
        lax.all_to_all(rows_out, "dp", split_axis=0, concat_axis=0, tiled=True),
        chosen,
        preferred_element_type=jnp.float32,
    )
    valid = token_positions[None, None, None, :] < lens[:, :, None, None]
    returned = return_maxima(jnp.max(jnp.where(valid, sim, -1e30), axis=-1))
    best = returned.reshape(page_owners * cap, qlen)[index]
    best = best.reshape(qry_dev, ncand, ppc, qlen)
    scores = jnp.sum(jnp.max(best, axis=2), axis=-1)
    return (vectors, scores)


def solution(mesh):
    in_specs = (
        P(("dp", "mp"), None, None),
        P("dp", "mp"),
        P("dp", "mp"),
        P("dp", "mp"),
        P("dp", None),
        P(),
        P("mp", "dp"),
        P("dp", "mp"),
        P("mp", "dp"),
        P(("dp", "mp"), None),
        P("dp", None, None),
        P("dp"),
        P(),
        P(("dp", "mp"), None, None),
    )
    out_specs = (P(("dp", "mp"), None, None), P(("dp", "mp"), None))
    return jax.shard_map(body, mesh=mesh, in_specs=in_specs, out_specs=out_specs, check_vma=False)
```

profile of v0, /device:TPU:0, one launch (start us, length us, event | category | flops | bytes accessed | tf_op | source)
XLA Modules:
  0.0 430.4 jit_solution(7618637017859715395)
XLA Ops:
  7.2 0.7 all-gather.4.cloned.1.call-update
  8.0 8.8 %all_gather.30 = bf16[8,32,1024]{2,1,0:T(8,128)(2,1)S(1)} all-gather(bf16[2,32,1024]{2,1,0:T(8,128)(2,1)} %param.14), channel_id=1, replica_groups=mesh['dp'=8,'mp'=4] {'mp'}, dimensions={0}, use_global_device_ids=true | all-gather | bytes 655360 | tf_op jit(solution)/shard_map/all_gather | solution.py:45
  16.8 32.9 %all_gather.32 = bf16[1024,256]{1,0:T(8,128)(2,1)S(1)} all-gather(bf16[128,256]{1,0:T(8,128)(2,1)} %param.15), channel_id=1, replica_groups=mesh['dp'=8,'mp'=4] {'dp'}, dimensions={0}, use_global_device_ids=true | all-gather | bytes 589824 | tf_op jit(solution)/shard_map/all_gather | solution.py:50
  50.2 31.5 %all_gather.33 = bf16[1024,256]{1,0:T(8,128)(2,1)S(1)} all-gather(bf16[128,256]{1,0:T(8,128)(2,1)S(1)} %copy-done.8), channel_id=1, replica_groups=mesh['dp'=8,'mp'=4] {'dp'}, dimensions={0}, use_global_device_ids=true | all-gather | bytes 589824 | tf_op jit(solution)/shard_map/all_gather | solution.py:51
  82.1 0.9 reshape.296
  83.0 31.5 %all_gather.31 = bf16[1024,256]{1,0:T(8,128)(2,1)S(1)} all-gather(bf16[128,256]{1,0:T(8,128)(2,1)S(1)} %copy-done.9), channel_id=1, replica_groups=mesh['dp'=8,'mp'=4] {'dp'}, dimensions={0}, use_global_device_ids=true | all-gather | bytes 589824 | tf_op jit(solution)/shard_map/all_gather | solution.py:52
  114.8 0.9 reshape.294
  115.7 27.0 %all_gather.35 = bf16[256,1024]{1,0:T(8,128)(2,1)S(1)} all-gather(bf16[256,128]{1,0:T(8,128)(2,1)S(1)} %copy-done.10), channel_id=1, replica_groups=mesh['dp'=8,'mp'=4] {'dp'}, dimensions={1}, use_global_device_ids=true | all-gather | bytes 589824 | tf_op jit(solution)/shard_map/all_gather | solution.py:82
  142.7 1.7 convolution_convert_fusion.4
  144.5 0.5 fusion.59
  145.2 1.4 fusion.3
  146.6 0.3 copy.44
  146.9 0.5 convolution_convert_fusion.3
  147.4 1.4 fusion.57
  148.9 1.4 fusion.1
  150.3 0.5 fusion.11
  151.7 1.1 convolution_convert_fusion
  152.9 0.7 all-gather.6.cloned.1.call-update
  153.6 0.5 all-gather.8.cloned.1.call-update
  154.4 1.1 gather_fusion
  155.6 17.8 %reduce-scatter.3.cloned.1.call-done = bf16[64,1024]{1,0:T(8,128)(2,1)} async-done(((bf16[256,1024]{1,0:T(8,128)(2,1)}), bf16[64,1024]{1,0:T(8,128)(2,1)}) %reduce-scatter.3.cloned.1.call-update) | async-done | bytes 131088 | tf_op jit(solution)/shard_map/reduce_scatter | solution.py:85
  173.4 1.0 fusion.67
  174.5 1.1 multiply_reduce_fusion.1
  175.6 1.0 divide_convert_fusion.3
  176.6 7.0 %all_gather.36 = bf16[256,1024]{1,0:T(8,128)(2,1)S(1)} all-gather(bf16[64,1024]{1,0:T(8,128)(2,1)S(1)} %divide_convert_fusion.3), channel_id=1, replica_groups=mesh['dp'=8,'mp'=4] {'mp'}, dimensions={0}, use_global_device_ids=true | all-gather | bytes 655360 | tf_op jit(solution)/shard_map/all_gather | solution.py:90
  183.6 41.5 %all-gather.6.cloned.1.call-done = bf16[1024,1024]{1,0:T(8,128)(2,1)} async-done(((bf16[128,1024]{1,0:T(8,128)(2,1)}), bf16[1024,1024]{1,0:T(8,128)(2,1)}) %all-gather.6.cloned.1.call-update) | async-done | bytes 2097168 | tf_op jit(solution)/shard_map/all_gather | solution.py:91
  225.1 51.7 %all-gather.8.cloned.1.call-done = bf16[1024,1024]{1,0:T(8,128)(2,1)} async-done(((bf16[1024,128]{1,0:T(8,128)(2,1)}), bf16[1024,1024]{1,0:T(8,128)(2,1)}) %all-gather.8.cloned.1.call-update) | async-done | bytes 2097168 | tf_op jit(solution)/shard_map/all_gather | solution.py:94
  276.8 6.5 %convolution_convert_fusion.1 = bf16[256,1024]{1,0:T(8,128)(2,1)} fusion(bf16[1024,1024]{1,0:T(8,128)(2,1)} %all-gather.8.cloned.1.call-done, bf16[256,1024]{1,0:T(8,128)(2,1)S(1)} %all_gather.36, bf16[1024,1024]{1,0:T(8,128)(2,1)} %all-gather.6.cloned.1.call-done), kind=kOutput, calls=%fused_computation.17 | convolution fusion | flops 1091043328 | bytes 5242880 | tf_op jit(solution)/shard_map/dot_general | solution.py:93
  283.8 1.0 scatter_custom_fusion
  284.8 0.7 all_to_all.14
  285.4 3.2 all-to-all-start
  288.7 42.6 %all_gather.39 = bf16[1024,128]{1,0:T(8,128)(2,1)S(1)} all-gather(bf16[32,128]{1,0:T(8,128)(2,1)S(1)} %copy-done.11), channel_id=1, replica_groups=mesh['dp'=8,'mp'=4] {'dp','mp'}, dimensions={0}, use_global_device_ids=true | all-gather | bytes 270336 | tf_op jit(solution)/shard_map/all_gather | solution.py:101
  331.3 1.0 fusion.65
  332.3 1.1 multiply_reduce_fusion
  333.4 1.3 multiply_reduce_fusion.2
  334.8 0.8 gather_fusion.2
  335.6 1.7 broadcast_in_dim.14
  337.3 13.7 %scatter_fusion = bf16[256,32,128]{2,1,0:T(8,128)(2,1)} fusion(bf16[256,32,128]{2,1,0:T(8,128)(2,1)} %broadcast_in_dim.14, s32[128]{0:T(128)S(1)} %fusion.75, bf16[128,32,128]{2,1,0:T(8,128)(2,1)S(1)} %gather_fusion.2), kind=kCustom, calls=%fused_computation.6 | custom fusion | bytes 3146240 | tf_op jit(solution)/shard_map/scatter | solution.py:125
  351.0 3.8 all-to-all-start.1
  354.9 11.8 %gather_fusion.3 = bf16[256,128,128]{2,1,0:T(8,128)(2,1)} fusion(bf16[256,128,128]{2,1,0:T(8,128)(2,1)} %param.24, s32[1024]{0:T(1024)S(1)} %pad_clamp_fusion.2), kind=kCustom, calls=%fused_computation.3 | custom fusion | bytes 16778240 | tf_op jit(solution)/shard_map/gather | solution.py:129
  366.7 1.9 gather_fusion.1
  368.8 34.7 %all-to-all-done.1 = bf16[8,32,32,128]{3,2,1,0:T(8,128)(2,1)S(1)} async-done(((bf16[8,32,32,128]{3,2,1,0:T(8,128)(2,1)}), bf16[8,32,32,128]{3,2,1,0:T(8,128)(2,1)S(1)}, u32[]{:S(2)}, u32[]{:S(2)}) %all-to-all-start.1) | async-done | bytes 2097184 | tf_op jit(solution)/shard_map/all_to_all | solution.py:133
  403.5 8.0 %select_reduce_fusion = bf16[8,32,32]{2,1,0:T(8,128)(2,1)S(1)} fusion(bf16[8,32,32,128]{3,2,1,0:T(8,128)(2,1)S(1)} %all-to-all-done.1, bf16[8,32,128,128]{3,2,1,0:T(8,128)(2,1)} %bitcast.84, pred[8,32,128]{2,1,0:T(8,128)(4,1)S(1)} %iota_compare_fusion.1), kind=kOutput, calls=%fused_computation.8 | convolution fusion | flops 270524416 | bytes 10534912 | tf_op jit(solution)/shard_map/snie,snte->snit/dot_general | solution.py:131
  411.5 0.7 reshape.372
  412.2 3.6 all-to-all-start.2
  415.8 6.6 %all-to-all-done.2 = bf16[8,2,512]{2,1,0:T(2,128)(2,1)S(1)} async-done(((bf16[8,2,512]{2,1,0:T(2,128)(2,1)}), bf16[8,2,512]{2,1,0:T(2,128)(2,1)S(1)}, u32[]{:S(2)}, u32[]{:S(2)}) %all-to-all-start.2) | async-done | bytes 16416 | tf_op jit(solution)/shard_map/all_to_all | solution.py:21
  422.5 0.6 gather_fusion.4
  423.2 0.7 reduce_sum.82
  (70 shorter events, 3.7 us)
Async XLA Ops:
  7.2 147.2 %copy-start = (s32[2048]{0:T(1024)S(1)}, s32[2048]{0:T(1024)}, u32[]{:S(2)}) copy-start(s32[2048]{0:T(1024)} %param.26) | copy-start | bytes 24580
  7.2 43.0 %copy-start.8 = (bf16[128,256]{1,0:T(8,128)(2,1)S(1)}, bf16[128,256]{1,0:T(8,128)(2,1)}, u32[]{:S(2)}) copy-start(bf16[128,256]{1,0:T(8,128)(2,1)} %param.16) | copy-start | bytes 196612
  7.2 135.5 %all-gather.4.cloned.1.call-start = ((), (), s32[]{:S(2)}) async-start(), calls=%async_computation.5 | async-start | bytes 1179648 | tf_op jit(solution)/shard_map/all_gather | solution.py:48
  7.9 165.5 %reduce-scatter.3.cloned.1.call-start = ((), (), s32[]{:S(2)}) async-start(), calls=%async_computation.6 | async-start | bytes 655360 | tf_op jit(solution)/shard_map/reduce_scatter | solution.py:85
  16.8 66.2 %copy-start.9 = (bf16[128,256]{1,0:T(8,128)(2,1)S(1)}, bf16[128,256]{1,0:T(8,128)(2,1)}, u32[]{:S(2)}) copy-start(bf16[128,256]{1,0:T(8,128)(2,1)} %param.17) | copy-start | bytes 196612
  50.2 65.5 %copy-start.10 = (bf16[256,128]{1,0:T(8,128)(2,1)S(1)}, bf16[256,128]{1,0:T(8,128)(2,1)}, u32[]{:S(2)}) copy-start(bf16[256,128]{1,0:T(8,128)(2,1)} %param.20) | copy-start | bytes 196612
  144.5 0.7 copy-start.7
  145.2 1.8 copy-start.3
  148.9 1.4 copy-start.5
  148.9 2.1 copy-start.6
  151.3 2.9 copy-start.12
  151.3 22.1 %copy-start.4 = (bf16[2,32,1024]{2,1,0:T(8,128)(2,1)S(1)}, bf16[2,32,1024]{2,1,0:T(8,128)(2,1)}, u32[]{:S(2)}) copy-start(bf16[2,32,1024]{2,1,0:T(8,128)(2,1)} %param.14) | copy-start | bytes 393220
  152.8 72.3 %all-gather.6.cloned.1.call-start = ((), (), s32[]{:S(2)}) async-start(), calls=%async_computation.7 | async-start | bytes 2359296 | tf_op jit(solution)/shard_map/all_gather | solution.py:91
  153.5 123.2 %all-gather.8.cloned.1.call-start = ((), (), s32[]{:S(2)}) async-start(), calls=%async_computation.8 | async-start | bytes 2359296 | tf_op jit(solution)/shard_map/all_gather | solution.py:94
  154.1 177.1 %reduce-scatter.5.cloned.1.call-start = ((), (), s32[]{:S(2)}) async-start(), calls=%async_computation.9 | async-start | bytes 655360 | tf_op jit(solution)/shard_map/reduce_scatter | solution.py:96
  183.6 105.1 %copy-start.11 = (bf16[32,128]{1,0:T(8,128)(2,1)S(1)}, bf16[32,128]{1,0:T(8,128)(2,1)}, u32[]{:S(2)}) copy-start(bf16[32,128]{1,0:T(8,128)(2,1)} %param.23) | copy-start | bytes 24580
  285.4 65.6 %all-to-all-start = ((s32[8,1,32]{2,1,0:T(1,128)}), s32[8,1,32]{2,1,0:T(1,128)S(1)}, u32[]{:S(2)}, u32[]{:S(2)}) async-start(s32[8,1,32]{2,1,0:T(1,128)} %all_to_all.14), calls=%async_computation.2 | async-start | bytes 8192 | tf_op jit(solution)/shard_map/all_to_all | solution.py:128
  334.8 2.4 copy-start.2
  351.0 52.5 %all-to-all-start.1 = ((bf16[8,32,32,128]{3,2,1,0:T(8,128)(2,1)}), bf16[8,32,32,128]{3,2,1,0:T(8,128)(2,1)S(1)}, u32[]{:S(2)}, u32[]{:S(2)}) async-start(bf16[8,32,32,128]{3,2,1,0:T(8,128)(2,1)} %bitcast.21), calls=%async_computation.3 | async-start | bytes 4194304 | tf_op jit(solution)/shard_map/all_to_all | solution.py:133
  354.9 11.8 %copy-start.1 = (s32[256]{0:T(256)S(1)}, s32[256]{0:T(256)}, u32[]{:S(2)}) copy-start(s32[256]{0:T(256)} %param.25) | copy-start | bytes 3076
  412.2 10.2 %all-to-all-start.2 = ((bf16[8,2,512]{2,1,0:T(2,128)(2,1)}), bf16[8,2,512]{2,1,0:T(2,128)(2,1)S(1)}, u32[]{:S(2)}, u32[]{:S(2)}) async-start(bf16[8,2,512]{2,1,0:T(2,128)(2,1)} %reshape.372), calls=%async_computation.4 | async-start | bytes 32768 | tf_op jit(solution)/shard_map/all_to_all | solution.py:21
Sparse Core Ops, SparseCore 0:
  10.2 46.8 all-gather.3
  152.9 20.4 reduce-scatter.2
  175.8 49.2 all-gather.5
  227.2 49.5 all-gather.7
  283.4 20.3 reduce-scatter.4
where the time goes:
time: 432 us; the launch traced here: 430 us
  blocking collectives  181 us (42%)
  waiting for transfers between devices  154 us (36%)
  local copies, waits for them, and re-layouts  37.4 us (9%)
  matrix products  25.4 us (6%)
  between operations  14.2 us (3%)
  starting transfers between devices  10.9 us (3%)
  other arithmetic  6.93 us (2%)
    all_gather x1, waiting for transfers between devices, body(): lax.all_gather(w_down, 'dp', axis=1, tiled=True)  51.7 us
    all_gather x1, blocking collectives, body(): lax.all_gather(w_proj, ('dp', 'mp'), axis=0, tiled=True)  42.6 us
    all_gather x1, waiting for transfers between devices, body(): up = add_rows(mid_all, lax.all_gather(w_up, 'dp', axis=0, tiled=True))  41.5 us
    all_to_all x1, waiting for transfers between devices, body(): lax.all_to_all(rows_out, 'dp', split_axis=0, concat_axis=0, tiled=True)  34.7 us
    all_gather x1, blocking collectives, body(): lax.all_gather(query_weight, 'dp', axis=0, tiled=True)  32.9 us
    all_gather x1, blocking collectives, body(): lax.all_gather(w_key, 'dp', axis=0, tiled=True)  31.5 us
    all_gather x1, blocking collectives, body(): lax.all_gather(w_value, 'dp', axis=0, tiled=True)  31.5 us
    all_gather x1, blocking collectives, body(): lax.all_gather(w_out, 'dp', axis=1, tiled=True)  27 us
  transfers between devices with their start and end apart: 8, of which 5 were waited for; matrix products, arithmetic and copies ran while one was open for 10% of the time, Pallas kernels for 0%

commit v1 on v0

v1 whole, which is shorter than its diff:
```python
import functools

import jax
import jax.numpy as jnp
from jax import lax
from jax.experimental import pallas as pl
from jax.experimental.pallas import tpu as pltpu
from jax.sharding import PartitionSpec as P

HD = 64
MESH = pl.DeviceIdType.MESH


def layer_norm(value):
    mean = jnp.mean(value, axis=-1, keepdims=True)
    centered = value - mean
    var = jnp.mean(centered * centered, axis=-1, keepdims=True)
    return centered / jnp.sqrt(var + 1e-07)


def add_rows(left, piece):
    return jnp.dot(left, piece, preferred_element_type=jnp.float32)


def gather_kernel(n, nm, count, *refs):
    hid, wp = refs[:2]
    ins = refs[2 : 2 + count]
    hid_out, wp_out = refs[2 + count : 4 + count]
    outs = refs[4 + count : 4 + 2 * count]
    wp_own, local_sem, mp_send, mp_recv, send_sem, recv_sem = refs[4 + 2 * count :]
    dp, mp = lax.axis_index("dp"), lax.axis_index("mp")
    half = n // 2
    row, col = dp // 2, dp % 2
    pos = row + col * (n - 1 - 2 * row)

    def at(p):
        p = (p + 2 * n) % n
        h = p // half
        return 2 * (p + h * (n - 1 - 2 * p)) + h

    right, left = at(pos + 1), at(pos - 1)
    barrier = pltpu.get_barrier_semaphore()
    for d in (left, right):
        pl.semaphore_signal(barrier, inc=1, device_id=(d, mp), device_id_type=MESH)
    for k in range(1, nm):
        pl.semaphore_signal(
            barrier, inc=1, device_id=(dp, (mp + k) % nm), device_id_type=MESH
        )
    pl.semaphore_wait(barrier, 2 + nm - 1)

    local = [pltpu.make_async_copy(wp, wp_own.at[mp], local_sem.at[0])]
    local.append(pltpu.make_async_copy(hid, hid_out.at[mp], local_sem.at[1]))
    for i in range(count):
        local.append(pltpu.make_async_copy(ins[i], outs[i].at[dp], local_sem.at[2 + i]))
    mp_copies = []
    for which, (src, dst) in enumerate(((wp, wp_own), (hid, hid_out))):
        for k in range(1, nm):
            copy = pltpu.make_async_remote_copy(
                src_ref=src,
                dst_ref=dst.at[mp],
                send_sem=mp_send.at[which, k - 1],
                recv_sem=mp_recv.at[which, k - 1],
                device_id=(dp, (mp + k) % nm),
                device_id_type=MESH,
            )
            copy.start()
            mp_copies.append(copy)

    all_outs = list(outs) + [wp_out]
    pending = {}

    def send(step, i, way):
        owner = at(pos - step) if way == 0 else at(pos + step)
        if i == count:
            h = nm // 2
            cut = pl.ds(way * h, h)
            src = wp_own.at[cut] if step == 0 else wp_out.at[owner, cut]
            dst = wp_out.at[owner, cut]
        else:
            src = ins[i].at[way] if step == 0 else outs[i].at[owner, way]
            dst = outs[i].at[owner, way]
        copy = pltpu.make_async_remote_copy(
            src_ref=src,
            dst_ref=dst,
            send_sem=send_sem.at[step, i, way],
            recv_sem=recv_sem.at[step, i, way],
            device_id=(right if way == 0 else left, mp),
            device_id_type=MESH,
        )
        copy.start()
        pending[step, i, way] = copy

    for step in range(n - 1):
        for i in range(count + 1):
            if step == 0 and i == count:
                for c in local:
                    c.start()
                local[0].wait()
                for c in mp_copies[: nm - 1]:
                    c.wait_recv()
                own = pltpu.make_async_copy(wp_own, wp_out.at[dp], local_sem.at[0])
                own.start()
            for way in range(2):
                if step:
                    pending[step - 1, i, way].wait_recv()
                send(step, i, way)
    for (step, i, way), copy in pending.items():
        if step == n - 2:
            copy.wait_recv()
    for c in mp_copies[nm - 1 :]:
        c.wait_recv()
    own.wait()
    for c in local[1:]:
        c.wait()
    for c in mp_copies:
        c.wait_send()
    for copy in pending.values():
        copy.wait_send()


def gather_all(n, nm, hidden, w_proj, arrays):
    arrays = [a.reshape((2, a.shape[0] // 2) + a.shape[1:]) for a in arrays]
    count = len(arrays)
    bf = jnp.bfloat16
    shapes = [
        jax.ShapeDtypeStruct((nm,) + hidden.shape, bf),
        jax.ShapeDtypeStruct((n, nm) + w_proj.shape, bf),
    ] + [jax.ShapeDtypeStruct((n,) + a.shape, bf) for a in arrays]
    out = pl.pallas_call(
        functools.partial(gather_kernel, n, nm, count),
        out_shape=shapes,
        in_specs=[pl.BlockSpec(memory_space=pl.ANY)] * (count + 2),
        out_specs=[pl.BlockSpec(memory_space=pl.ANY)] * (count + 2),
        scratch_shapes=[
            pltpu.VMEM((nm,) + w_proj.shape, bf),
            pltpu.SemaphoreType.DMA((count + 2,)),
            pltpu.SemaphoreType.DMA((2, nm - 1)),
            pltpu.SemaphoreType.DMA((2, nm - 1)),
            pltpu.SemaphoreType.DMA((n - 1, count + 1, 2)),
            pltpu.SemaphoreType.DMA((n - 1, count + 1, 2)),
        ],
        compiler_params=pltpu.CompilerParams(collective_id=0, has_side_effects=True),
    )(hidden, w_proj, *arrays)
    flat = [o.reshape((n, o.shape[1] * o.shape[2]) + o.shape[3:]) for o in out[2:]]
    return out[0], out[1], flat


def score_kernel(n, cap, rows, where_ref, lens_ref, vec_ref, pages_ref, out_ref, buf, sems):
    ptok = buf.shape[2]
    group = 8

    def page_copy(s, r):
        return pltpu.make_async_copy(
            pages_ref.at[where_ref[s * cap + r]], buf.at[s, r], sems.at[s]
        )

    def start(s, carry):
        for r in range(cap):
            page_copy(s, r).start()
        return carry

    lax.fori_loop(0, n, start, 0)
    token = lax.broadcasted_iota(jnp.int32, (ptok, rows), 0)

    def work(s, carry):
        pltpu.make_async_copy(buf.at[s], buf.at[s], sems.at[s]).wait()
        vec = vec_ref[s]
        for g in range(cap // group):
            chunk = buf[s, pl.ds(g * group, group)].reshape(group * ptok, -1)
            sim = lax.dot_general(
                chunk, vec, (((1,), (1,)), ((), ())), preferred_element_type=jnp.float32
            )
            best = []
            for r in range(group):
                length = lens_ref[where_ref[s * cap + g * group + r]]
                part = sim[r * ptok : (r + 1) * ptok]
                part = jnp.where(token < length, part, -1e30)
                best.append(jnp.max(part, axis=0, keepdims=True))
            out_ref[s, pl.ds(g * group, group)] = jnp.concatenate(best, axis=0)
        return carry

    lax.fori_loop(0, n, work, 0)


def score_pages(where, lens, vecs, pages):
    n, cap = where.shape
    rows = vecs.shape[1]
    grid_spec = pltpu.PrefetchScalarGridSpec(
        num_scalar_prefetch=2,
        grid=(1,),
        in_specs=[
            pl.BlockSpec(vecs.shape, lambda i, a, b: (0, 0, 0)),
            pl.BlockSpec(memory_space=pl.ANY),
        ],
        out_specs=pl.BlockSpec((n, cap, rows), lambda i, a, b: (0, 0, 0)),
        scratch_shapes=[
            pltpu.VMEM((n, cap) + pages.shape[1:], pages.dtype),
            pltpu.SemaphoreType.DMA((n,)),
        ],
    )
    return pl.pallas_call(
        functools.partial(score_kernel, n, cap, rows),
        grid_spec=grid_spec,
        out_shape=jax.ShapeDtypeStruct((n, cap, rows), jnp.float32),
        compiler_params=pltpu.CompilerParams(vmem_limit_bytes=40 * 2**20),
    )(where.reshape(-1), lens, vecs, pages)


def body(
    hidden,
    query_weight,
    w_key,
    w_value,
    rel_table,
    rel_bucket,
    w_out,
    w_up,
    w_down,
    w_proj,
    pages,
    page_len,
    slot_per_page,
    candidates,
):
    n, nm = lax.axis_size("dp"), lax.axis_size("mp")
    qry_dev, qlen, width = hidden.shape
    heads_local = query_weight.shape[1] // HD
    cols = query_weight.shape[1]

    pg_dev = pages.shape[0]
    ncand, ppc = (candidates.shape[1], candidates.shape[2])
    req = qry_dev * ncand * ppc
    cap = 2 * req // n
    slots = slot_per_page[candidates.reshape(req)]
    dest = slots // pg_dev
    order = jnp.arange(req, dtype=jnp.int32)
    earlier = (dest[:, None] == dest[None, :]) & (order[None, :] < order[:, None])
    place = jnp.sum(earlier.astype(jnp.int32), axis=1)
    index = dest * cap + place
    codes = jnp.zeros((n * cap,), jnp.int32).at[index].set(slots % pg_dev)
    where_local = lax.all_to_all(
        codes.reshape(n, cap), "dp", split_axis=0, concat_axis=0, tiled=True
    )

    tokens, proj_w, (wq, wk, wv, rel, wo, wu, wd) = gather_all(
        n,
        nm,
        hidden.reshape(qry_dev * qlen, width),
        w_proj,
        (query_weight, w_key, w_value, rel_table, w_out, w_up, w_down),
    )
    group = nm * qry_dev
    flat = tokens.reshape(group * qlen, width)
    wq, wk, wv = (w.reshape(width, cols) for w in (wq, wk, wv))
    rel = rel.reshape(-1, width)
    wo = jnp.transpose(wo, (1, 0, 2)).reshape(wo.shape[1], width)
    wd = jnp.transpose(wd, (1, 0, 2)).reshape(wd.shape[1], width)
    wu = wu.reshape(width, -1)
    qsum = add_rows(flat, wq)
    ksum = add_rows(flat, wk)
    vsum = add_rows(flat, wv)
    rel_q = add_rows(rel, wq).astype(jnp.bfloat16)
    rel_k = add_rows(rel, wk).astype(jnp.bfloat16)
    nbuck = rel_q.shape[0]
    qx = qsum.astype(jnp.bfloat16).reshape(group, qlen, heads_local, HD)
    kx = ksum.astype(jnp.bfloat16).reshape(group, qlen, heads_local, HD)
    vx = vsum.astype(jnp.bfloat16).reshape(group, qlen, heads_local, HD)
    rel_q = rel_q.reshape(nbuck, heads_local, HD)
    rel_k = rel_k.reshape(nbuck, heads_local, HD)
    onehot = (rel_bucket[:, :, None] == jnp.arange(nbuck, dtype=jnp.int32)[None, None, :]).astype(
        jnp.float32
    )
    scale = 1.0 / jnp.sqrt(jnp.float32(3 * HD))
    content = jnp.einsum("qihd,qjhd->qhij", qx, kx, preferred_element_type=jnp.float32)
    along_axis_name = jnp.einsum("qihd,bhd->qhib", qx, rel_k, preferred_element_type=jnp.float32)
    c2p = jnp.einsum("qhib,ijb->qhij", along_axis_name, onehot, precision=lax.Precision.HIGHEST)
    back = jnp.einsum("qjhd,bhd->qhjb", kx, rel_q, preferred_element_type=jnp.float32)
    p2c = jnp.einsum("qhjb,jib->qhij", back, onehot, precision=lax.Precision.HIGHEST)
    logits = (content + c2p + p2c) * scale
    probs = jax.nn.softmax(logits, axis=-1).astype(jnp.bfloat16)
    context_rows = jnp.einsum("qhij,qjhd->qihd", probs, vx, preferred_element_type=jnp.float32)
    context_rows = context_rows.astype(jnp.bfloat16).reshape(group * qlen, cols)
    attn_terms = add_rows(context_rows, wo)
    attn = lax.psum_scatter(
        attn_terms.astype(jnp.bfloat16), "mp", scatter_dimension=0, tiled=True
    ).astype(jnp.float32)
    own = hidden.reshape(qry_dev * qlen, width).astype(jnp.float32)
    mid = layer_norm(own + attn).astype(jnp.bfloat16)
    mid_all = lax.all_gather(mid, "mp", axis=0, tiled=True)
    up = add_rows(mid_all, wu)
    inner = jax.nn.gelu(up, approximate=False).astype(jnp.bfloat16)
    down_terms = add_rows(inner, wd)
    mlp = lax.psum_scatter(
        down_terms.astype(jnp.bfloat16), "mp", scatter_dimension=0, tiled=True
    ).astype(jnp.float32)
    state = layer_norm(mid.astype(jnp.float32) + mlp).astype(jnp.bfloat16)
    width_out = w_proj.shape[1]
    proj = add_rows(state, proj_w.reshape(width, width_out))
    vectors = (proj / jnp.sqrt(jnp.sum(proj * proj, axis=-1, keepdims=True) + 1e-06)).astype(
        jnp.bfloat16
    )
    spread = jnp.broadcast_to(vectors[None], (n,) + vectors.shape)
    seen = lax.all_to_all(spread, "dp", split_axis=0, concat_axis=0, tiled=True)
    best = score_pages(where_local, page_len, seen, pages).astype(jnp.bfloat16)
    back_home = lax.all_to_all(best, "dp", split_axis=0, concat_axis=0, tiled=True)
    best = back_home.reshape(n * cap, qry_dev * qlen)[index].astype(jnp.float32)
    best = best.reshape(qry_dev, ncand, ppc, qry_dev, qlen)
    best = jnp.stack([best[q, :, :, q] for q in range(qry_dev)])
    scores = jnp.sum(jnp.max(best, axis=2), axis=-1)
    return (vectors.reshape(qry_dev, qlen, width_out), scores)


def solution(mesh):
    in_specs = (
        P(("dp", "mp"), None, None),
        P("dp", "mp"),
        P("dp", "mp"),
        P("dp", "mp"),
        P("dp", None),
        P(),
        P("mp", "dp"),
        P("dp", "mp"),
        P("mp", "dp"),
        P(("dp", "mp"), None),
        P("dp", None, None),
        P("dp"),
        P(),
        P(("dp", "mp"), None, None),
    )
    out_specs = (P(("dp", "mp"), None, None), P(("dp", "mp"), None))
    return jax.shard_map(body, mesh=mesh, in_specs=in_specs, out_specs=out_specs, check_vma=False)
```

time: 432 us -> 220 us (0.51)
  blocking collectives: 181 us -> 6.95 us
  waiting for transfers between devices: 154 us -> 44.9 us
  Pallas kernels: 0 us -> 95.9 us
  local copies, waits for them, and re-layouts: 37.4 us -> 15.6 us
  matrix products: 25.4 us -> 19.9 us
    all_gather x6 -> x0, blocking collectives: 174 us -> none  [the longest x1 42.6 us: body(): lax.all_gather(w_proj, ('dp', 'mp'), axis=0, tiled=True)]
    pallas_call x0 -> x2, Pallas kernels: none -> 95.9 us  [the longest x1 79.6 us: gather_all(): pl.pallas_call(functools.partial(gather_kernel, n, nm, count), out_shape=...]
    all_gather x3 -> x0, waiting for transfers between devices: 93.2 us -> none  [the longest x1 51.7 us: body(): lax.all_gather(w_down, 'dp', axis=1, tiled=True)]
    all_to_all x3, waiting for transfers between devices: 41.3 us -> 12.7 us  [the longest x1 6.61 us: body(): lax.all_to_all(best, 'dp', split_axis=0, concat_axis=0, tiled=True)]
    dot_general x3 -> x0, matrix products: 15.5 us -> none  [the longest x1 7.96 us: body(): jnp.einsum('snie,snte->snit', lax.all_to_all(rows_out, 'dp', split_axis=0...]
    gather x5 -> x1, local copies, waits for them, and re-layouts: 15.2 us -> 0.71 us  [body(): best = back_home.reshape(n * cap, qry_dev * qlen)[index].astype(jnp.float32)]
    scatter x2 -> x1, local copies, waits for them, and re-layouts: 14.7 us -> 0.98 us  [body(): codes = jnp.zeros((n * cap,), jnp.int32).at[index].set(slots % pg_dev)]
    reduce_scatter x1, waiting for transfers between devices: 0.01 us -> 13.4 us  [body(): lax.psum_scatter(down_terms.astype(jnp.bfloat16), 'mp', scatter_dimension...]
  transfers between devices with their start and end apart: 8 -> 5, of which waited for: 5 -> 4; matrix products, arithmetic and copies ran while one was open for 10% -> 5% of each run, Pallas kernels for 0% -> 0%
where the time goes in v1:
time: 220 us; the launch traced here: 219 us
  Pallas kernels  95.9 us (44%)
  waiting for transfers between devices  44.9 us (20%)
  matrix products  19.9 us (9%)
  local copies, waits for them, and re-layouts  15.6 us (7%)
  between operations  14.5 us (7%)
  starting transfers between devices  14.4 us (7%)
  other arithmetic  7.2 us (3%)
  blocking collectives  6.95 us (3%)
    pallas_call x1, Pallas kernels, gather_all(): pl.pallas_call(functools.partial(gather_kernel, n, nm, count), out_shape=...  79.6 us
    reduce_scatter x1, waiting for transfers between devices, body(): lax.psum_scatter(attn_terms.astype(jnp.bfloat16), 'mp', scatter_dimension...  18.7 us
    pallas_call x1, Pallas kernels, score_pages(): pl.pallas_call(functools.partial(score_kernel, n, cap, rows), grid_spec=g...  16.3 us
    reduce_scatter x1, waiting for transfers between devices, body(): lax.psum_scatter(down_terms.astype(jnp.bfloat16), 'mp', scatter_dimension...  13.4 us
    dot_general x8, matrix products, add_rows(): return jnp.dot(left, piece, preferred_element_type=jnp.float32)  13.3 us
    all_gather x1, blocking collectives, body(): mid_all = lax.all_gather(mid, 'mp', axis=0, tiled=True)  6.95 us
    all_to_all x1, waiting for transfers between devices, body(): lax.all_to_all(best, 'dp', split_axis=0, concat_axis=0, tiled=True)  6.61 us
    all_to_all x1, waiting for transfers between devices, body(): seen = lax.all_to_all(spread, 'dp', split_axis=0, concat_axis=0, tiled=True)  6.09 us
  transfers between devices with their start and end apart: 5, of which 4 were waited for; matrix products, arithmetic and copies ran while one was open for 5% of the time, Pallas kernels for 0%

profile of v1, /device:TPU:0, one launch (start us, length us, event | category | flops | bytes accessed | tf_op | source)
XLA Modules:
  0.0 219.3 jit_solution(14706121458980288904)
XLA Ops:
  7.2 79.6 %shard_map.149 = (bf16[4,64,1024]{2,1,0:T(8,128)(2,1)}, bf16[8,4,32,128]{3,2,1,0:T(8,128)(2,1)}, bf16[8,2,64,256]{3,2,1,0:T(8,128)(2,1)}, bf16[8,2,64,256]{3,2,1...) custom-call(bf16[64,1024]{1,0:T(8,128)(2,1)} %bitcast.107, ...), custom_call_target="tpu_custom_call" | custom-call | tf_op jit(solution)/shard_map/pallas_call | solution.py:129
  86.8 1.6 convolution_convert_fusion.5
  88.5 1.5 convolution_convert_fusion.6
  90.0 0.5 convolution_convert_fusion.3
  90.5 0.5 convolution_convert_fusion.4
  91.2 0.3 convolution_convert_fusion.7
  92.0 0.2 copy.44
  92.3 0.5 fusion.57
  92.7 0.2 copy-done.12
  93.0 1.4 fusion.1
  94.4 0.5 fusion.59
  94.8 1.4 fusion.3
  96.3 0.3 copy.38
  96.6 0.4 fusion.11
  97.1 0.8 copy-done.11
  97.8 0.2 fusion.106
  98.0 2.4 %fusion.12 = bf16[8,32,4,64]{3,1,2,0:T(8,128)(2,1)} fusion(bf16[8,32,4,64]{3,2,1,0:T(4,128)(2,1)S(1)} %reshape.244, f32[8,4,32]{2,1,0:T(4,128)S(1)} %fusion.106, f32[8,4,32,32]{2,3,1,0:T(8,128)} %copy-done.11), kind=kOutput, calls=%fused_computation.21 | convolution fusion | flops 4359199 | bytes 397312 | tf_op jit(solution)/shard_map/qhij,qjhd->qihd/dot_general | solution.py:281
  100.4 1.1 copy.43
  101.5 0.2 reshape.249
  101.7 1.1 convolution_convert_fusion
  103.0 2.6 %copy.45 = bf16[8,1024,128]{1,2,0:T(8,128)(2,1)} copy(bf16[8,1024,128]{2,1,0:T(8,128)(2,1)S(1)} %bitcast.104) | data formatting | bytes 4194304 | tf_op jit(solution)/shard_map/reshape | solution.py:144
  105.6 18.7 %reduce-scatter.3.cloned.1.call-done = bf16[64,1024]{1,0:T(8,128)(2,1)} async-done(((bf16[256,1024]{1,0:T(8,128)(2,1)}), bf16[64,1024]{1,0:T(8,128)(2,1)}) %reduce-scatter.3.cloned.1.call-update) | async-done | bytes 131088 | tf_op jit(solution)/shard_map/reduce_scatter | solution.py:284
  124.3 1.0 fusion.65
  125.4 1.1 multiply_reduce_fusion.1
  126.5 1.0 divide_convert_fusion.3
  127.5 6.9 %all_gather.3 = bf16[256,1024]{1,0:T(8,128)(2,1)S(1)} all-gather(bf16[64,1024]{1,0:T(8,128)(2,1)S(1)} %divide_convert_fusion.3), channel_id=1, replica_groups=mesh['dp'=8,'mp'=4] {'mp'}, dimensions={0}, use_global_device_ids=true | all-gather | bytes 655360 | tf_op jit(solution)/shard_map/all_gather | solution.py:289
  134.5 6.5 %convolution_convert_fusion.1 = bf16[256,1024]{1,0:T(8,128)(2,1)} fusion(bf16[1024,1024]{0,1:T(8,128)(2,1)} %bitcast.105, bf16[256,1024]{1,0:T(8,128)(2,1)S(1)} %all_gather.3, bf16[1024,1024]{1,0:T(8,128)(2,1)} %bitcast.123), kind=kOutput, calls=%fused_computation.12 | convolution fusion | flops 1091043328 | bytes 5242880 | tf_op jit(solution)/shard_map/dot_general | solution.py:22
  141.3 1.1 gather_fusion
  142.4 0.2 convert_reduce_fusion
  142.6 1.0 scatter_custom_fusion
  143.6 0.7 all_to_all.12
  144.3 5.5 %all-to-all-start = ((s32[8,1,32]{2,1,0:T(1,128)}), s32[8,1,32]{2,1,0:T(1,128)S(1)}, u32[]{:S(2)}, u32[]{:S(2)}) async-start(s32[8,1,32]{2,1,0:T(1,128)} %all_to_all.12), calls=%async_computation.2 | async-start | bytes 8192 | tf_op jit(solution)/shard_map/all_to_all | solution.py:241
  149.8 13.4 %reduce-scatter.5.cloned.1.call-done = bf16[64,1024]{1,0:T(8,128)(2,1)} async-done(((bf16[256,1024]{1,0:T(8,128)(2,1)}), bf16[64,1024]{1,0:T(8,128)(2,1)}) %reduce-scatter.5.cloned.1.call-update) | async-done | bytes 131088 | tf_op jit(solution)/shard_map/reduce_scatter | solution.py:293
  163.2 1.0 fusion.67
  164.3 1.1 multiply_reduce_fusion
  165.4 1.3 multiply_reduce_fusion.2
  166.8 0.7 broadcast_in_dim.5
  167.5 5.5 %all-to-all-start.1 = ((bf16[8,64,128]{2,1,0:T(8,128)(2,1)}), bf16[8,64,128]{2,1,0:T(8,128)(2,1)S(1)}, u32[]{:S(2)}, u32[]{:S(2)}) async-start(bf16[8,64,128]{2,1,0:T(8,128)(2,1)} %broadcast_in_dim.5), calls=%async_computation.3 | async-start | bytes 262144 | tf_op jit(solution)/shard_map/all_to_all | solution.py:303
  173.0 0.5 broadcast.229
  173.5 0.7 reduce.3
  174.3 6.1 %all-to-all-done.1.vec_ref = bf16[8,64,128]{2,1,0:T(8,128)(2,1)S(1)} async-done(((bf16[8,64,128]{2,1,0:T(8,128)(2,1)}), bf16[8,64,128]{2,1,0:T(8,128)(2,1)S(1)}, u32[]{:S(2)}, u32[]{:S(2)}) %all-to-all-start.1) | async-done | bytes 131104 | tf_op jit(solution)/shard_map/all_to_all | solution.py:303
  180.3 3.4 %copy-done.1 = bf16[256,128,128]{2,1,0:T(8,128)(2,1)S(1)} copy-done((bf16[256,128,128]{2,1,0:T(8,128)(2,1)S(1)}, bf16[256,128,128]{2,1,0:T(8,128)(2,1)}, u32[]{:S(2)}) %copy-start.1) | copy-done | bytes 8388632
  183.7 16.3 %shard_map.150 = f32[8,32,64]{2,1,0:T(8,128)S(1)} custom-call(s32[256]{0:T(256)S(1)} %reshape.257.where_ref, s32[256]{0:T(256)S(1)} %copy-done.2, bf16[8,64,128]{2,1,0:T(8,128)(2,1)S(1)} %all-to-all-done.1.vec_ref, bf16[256,128,128]{2,1,0:T(8,128)(2,1)S(1)} %copy-done.1), custom_call_target="tpu_custom_call" | custom-call | tf_op jit(solution)/shard_map/pallas_call | solution.py:201
  200.1 0.7 reshape.298
  200.8 3.3 %all-to-all-start.2 = ((bf16[8,2,1024]{2,1,0:T(2,128)(2,1)}), bf16[8,2,1024]{2,1,0:T(2,128)(2,1)S(1)}, u32[]{:S(2)}, u32[]{:S(2)}) async-start(bf16[8,2,1024]{2,1,0:T(2,128)(2,1)} %reshape.298), calls=%async_computation.4 | async-start | bytes 65536 | tf_op jit(solution)/shard_map/all_to_all | solution.py:305
  204.1 6.6 %all-to-all-done.2 = bf16[8,2,1024]{2,1,0:T(2,128)(2,1)S(1)} async-done(((bf16[8,2,1024]{2,1,0:T(2,128)(2,1)}), bf16[8,2,1024]{2,1,0:T(2,128)(2,1)S(1)}, u32[]{:S(2)}, u32[]{:S(2)}) %all-to-all-start.2) | async-done | bytes 32800 | tf_op jit(solution)/shard_map/all_to_all | solution.py:305
  210.9 0.7 gather_fusion.1
  211.8 0.7 reduce_sum.82
  (56 shorter events, 1.6 us)
Async XLA Ops:
  7.2 134.1 %copy-start = (s32[2048]{0:T(1024)S(1)}, s32[2048]{0:T(1024)}, u32[]{:S(2)}) copy-start(s32[2048]{0:T(1024)} %param.26) | copy-start | bytes 24580
  7.2 117.1 %reduce-scatter.3.cloned.1.call-start = ((), (), s32[]{:S(2)}) async-start(), calls=%async_computation.5 | async-start | bytes 655360 | tf_op jit(solution)/shard_map/reduce_scatter | solution.py:284
  86.8 3.2 %copy-start.4 = (bf16[8,2,32,1024]{3,2,1,0:T(8,128)(2,1)S(1)}, bf16[8,2,32,1024]{3,2,1,0:T(8,128)(2,1)}, u32[]{:S(2)}) copy-start(bf16[8,2,32,1024]{3,2,1,0:T(8,128)(2,1)} %get-tuple-element.15) | copy-start | bytes 3145732
  86.8 3.2 %copy-start.6 = (bf16[8,2,64,256]{3,2,1,0:T(8,128)(2,1)S(1)}, bf16[8,2,64,256]{3,2,1,0:T(8,128)(2,1)}, u32[]{:S(2)}) copy-start(bf16[8,2,64,256]{3,2,1,0:T(8,128)(2,1)} %get-tuple-element.13) | copy-start | bytes 1572868
  86.8 3.7 %copy-start.5 = (bf16[8,2,64,256]{3,2,1,0:T(8,128)(2,1)S(1)}, bf16[8,2,64,256]{3,2,1,0:T(8,128)(2,1)}, u32[]{:S(2)}) copy-start(bf16[8,2,64,256]{3,2,1,0:T(8,128)(2,1)} %get-tuple-element.14) | copy-start | bytes 1572868
  90.0 1.0 copy-start.3
  90.0 1.2 copy-start.10
  90.5 1.5 copy-start.9
  92.2 0.7 copy-start.12
  97.1 0.8 copy-start.11
  98.0 4.9 %copy-start.7 = (bf16[8,2,512,128]{3,2,1,0:T(8,128)(2,1)S(1)}, bf16[8,2,512,128]{3,2,1,0:T(8,128)(2,1)}, u32[]{:S(2)}) copy-start(bf16[8,2,512,128]{3,2,1,0:T(8,128)(2,1)} %get-tuple-element.18) | copy-start | bytes 6291460
  102.9 60.3 %reduce-scatter.5.cloned.1.call-start = ((), (), s32[]{:S(2)}) async-start(), calls=%async_computation.6 | async-start | bytes 655360 | tf_op jit(solution)/shard_map/reduce_scatter | solution.py:293
  103.0 21.4 %copy-start.8 = (bf16[2,32,1024]{2,1,0:T(8,128)(2,1)S(1)}, bf16[2,32,1024]{2,1,0:T(8,128)(2,1)}, u32[]{:S(2)}) copy-start(bf16[2,32,1024]{2,1,0:T(8,128)(2,1)} %param.14) | copy-start | bytes 393220
  134.4 6.6 %copy-start.14 = (s32[2,16,4]{1,2,0:T(4,128)S(1)}, s32[2,16,4]{1,2,0:T(4,128)}, u32[]{:S(2)}) copy-start(s32[2,16,4]{1,2,0:T(4,128)} %param.27) | copy-start | bytes 1540
  134.5 31.0 %copy-start.15 = (bf16[8,4,32,128]{3,2,1,0:T(8,128)(2,1)S(1)}, bf16[8,4,32,128]{3,2,1,0:T(8,128)(2,1)}, u32[]{:S(2)}) copy-start(bf16[8,4,32,128]{3,2,1,0:T(8,128)(2,1)} %get-tuple-element.19) | copy-start | bytes 786436
  141.0 39.4 %copy-start.2 = (s32[256]{0:T(256)S(1)}, s32[256]{0:T(256)}, u32[]{:S(2)}) copy-start(s32[256]{0:T(256)} %lens_ref.1) | copy-start | bytes 3076
  144.3 22.5 %all-to-all-start = ((s32[8,1,32]{2,1,0:T(1,128)}), s32[8,1,32]{2,1,0:T(1,128)S(1)}, u32[]{:S(2)}, u32[]{:S(2)}) async-start(s32[8,1,32]{2,1,0:T(1,128)} %all_to_all.12), calls=%async_computation.2 | async-start | bytes 8192 | tf_op jit(solution)/shard_map/all_to_all | solution.py:241
  166.8 33.2 %copy-start.13 = (bf16[64,128]{1,0:T(8,128)(2,1)}, bf16[64,128]{1,0:T(8,128)(2,1)S(1)}, u32[]{:S(2)}) copy-start(bf16[64,128]{1,0:T(8,128)(2,1)S(1)} %divide_convert_fusion.5) | copy-start | bytes 49156
  167.5 12.9 %all-to-all-start.1 = ((bf16[8,64,128]{2,1,0:T(8,128)(2,1)}), bf16[8,64,128]{2,1,0:T(8,128)(2,1)S(1)}, u32[]{:S(2)}, u32[]{:S(2)}) async-start(bf16[8,64,128]{2,1,0:T(8,128)(2,1)} %broadcast_in_dim.5), calls=%async_computation.3 | async-start | bytes 262144 | tf_op jit(solution)/shard_map/all_to_all | solution.py:303
  180.3 3.4 %copy-start.1 = (bf16[256,128,128]{2,1,0:T(8,128)(2,1)S(1)}, bf16[256,128,128]{2,1,0:T(8,128)(2,1)}, u32[]{:S(2)}) copy-start(bf16[256,128,128]{2,1,0:T(8,128)(2,1)} %pages_ref.1) | copy-start | bytes 25165828
  200.8 10.0 %all-to-all-start.2 = ((bf16[8,2,1024]{2,1,0:T(2,128)(2,1)}), bf16[8,2,1024]{2,1,0:T(2,128)(2,1)S(1)}, u32[]{:S(2)}, u32[]{:S(2)}) async-start(bf16[8,2,1024]{2,1,0:T(2,128)(2,1)} %reshape.298), calls=%async_computation.4 | async-start | bytes 65536 | tf_op jit(solution)/shard_map/all_to_all | solution.py:305
Sparse Core Ops, SparseCore 0:
  103.0 21.2 reduce-scatter.2
  141.1 22.0 reduce-scatter.4

commit v2 on v1

--- a/solution.py
+++ b/solution.py
@@ -23,11 +23,13 @@
 
 
 def gather_kernel(n, nm, count, *refs):
-    hid, wp = refs[:2]
-    ins = refs[2 : 2 + count]
-    hid_out, wp_out = refs[2 + count : 4 + count]
-    outs = refs[4 + count : 4 + 2 * count]
-    wp_own, local_sem, mp_send, mp_recv, send_sem, recv_sem = refs[4 + 2 * count :]
+    hid, wp, codes = refs[:3]
+    ins = refs[3 : 3 + count]
+    hid_out, wp_out, codes_out = refs[3 + count : 6 + count]
+    outs = refs[6 + count : 6 + 2 * count]
+    wp_own, local_sem, mp_send, mp_recv, code_send, code_recv, send_sem, recv_sem = refs[
+        6 + 2 * count :
+    ]
     dp, mp = lax.axis_index("dp"), lax.axis_index("mp")
     half = n // 2
     row, col = dp // 2, dp % 2
@@ -40,13 +42,15 @@
 
     right, left = at(pos + 1), at(pos - 1)
     barrier = pltpu.get_barrier_semaphore()
-    for d in (left, right):
-        pl.semaphore_signal(barrier, inc=1, device_id=(d, mp), device_id_type=MESH)
+    for k in range(1, n):
+        pl.semaphore_signal(
+            barrier, inc=1, device_id=((dp + k) % n, mp), device_id_type=MESH
+        )
     for k in range(1, nm):
         pl.semaphore_signal(
             barrier, inc=1, device_id=(dp, (mp + k) % nm), device_id_type=MESH
         )
-    pl.semaphore_wait(barrier, 2 + nm - 1)
+    pl.semaphore_wait(barrier, n - 1 + nm - 1)
 
     local = [pltpu.make_async_copy(wp, wp_own.at[mp], local_sem.at[0])]
     local.append(pltpu.make_async_copy(hid, hid_out.at[mp], local_sem.at[1]))
@@ -66,7 +70,19 @@
             copy.start()
             mp_copies.append(copy)
 
-    all_outs = list(outs) + [wp_out]
+    local.append(pltpu.make_async_copy(codes.at[dp], codes_out.at[dp], local_sem.at[2 + count]))
+    code_copies = []
+    for k in range(1, n):
+        copy = pltpu.make_async_remote_copy(
+            src_ref=codes.at[(dp + k) % n],
+            dst_ref=codes_out.at[dp],
+            send_sem=code_send.at[k - 1],
+            recv_sem=code_recv.at[k - 1],
+            device_id=((dp + k) % n, mp),
+            device_id_type=MESH,
+        )
+        copy.start()
+        code_copies.append(copy)
     pending = {}
 
     def send(step, i, way):
@@ -109,6 +125,8 @@
             copy.wait_recv()
     for c in mp_copies[nm - 1 :]:
         c.wait_recv()
+    for c in code_copies:
+        c.wait()
     own.wait()
     for c in local[1:]:
         c.wait()
@@ -118,92 +136,242 @@
         copy.wait_send()
 
 
-def gather_all(n, nm, hidden, w_proj, arrays):
+def gather_all(n, nm, hidden, w_proj, codes, arrays):
     arrays = [a.reshape((2, a.shape[0] // 2) + a.shape[1:]) for a in arrays]
     count = len(arrays)
     bf = jnp.bfloat16
     shapes = [
         jax.ShapeDtypeStruct((nm,) + hidden.shape, bf),
         jax.ShapeDtypeStruct((n, nm) + w_proj.shape, bf),
+        jax.ShapeDtypeStruct(codes.shape, jnp.int32),
     ] + [jax.ShapeDtypeStruct((n,) + a.shape, bf) for a in arrays]
     out = pl.pallas_call(
         functools.partial(gather_kernel, n, nm, count),
         out_shape=shapes,
-        in_specs=[pl.BlockSpec(memory_space=pl.ANY)] * (count + 2),
-        out_specs=[pl.BlockSpec(memory_space=pl.ANY)] * (count + 2),
+        in_specs=[pl.BlockSpec(memory_space=pl.ANY)] * (count + 3),
+        out_specs=[pl.BlockSpec(memory_space=pl.ANY)] * (count + 3),
         scratch_shapes=[
             pltpu.VMEM((nm,) + w_proj.shape, bf),
-            pltpu.SemaphoreType.DMA((count + 2,)),
+            pltpu.SemaphoreType.DMA((count + 3,)),
             pltpu.SemaphoreType.DMA((2, nm - 1)),
             pltpu.SemaphoreType.DMA((2, nm - 1)),
+            pltpu.SemaphoreType.DMA((n - 1,)),
+            pltpu.SemaphoreType.DMA((n - 1,)),
             pltpu.SemaphoreType.DMA((n - 1, count + 1, 2)),
             pltpu.SemaphoreType.DMA((n - 1, count + 1, 2)),
         ],
         compiler_params=pltpu.CompilerParams(collective_id=0, has_side_effects=True),
-    )(hidden, w_proj, *arrays)
-    flat = [o.reshape((n, o.shape[1] * o.shape[2]) + o.shape[3:]) for o in out[2:]]
-    return out[0], out[1], flat
-
-
-def score_kernel(n, cap, rows, where_ref, lens_ref, vec_ref, pages_ref, out_ref, buf, sems):
-    ptok = buf.shape[2]
-    group = 8
-
-    def page_copy(s, r):
-        return pltpu.make_async_copy(
-            pages_ref.at[where_ref[s * cap + r]], buf.at[s, r], sems.at[s]
-        )
-
-    def start(s, carry):
-        for r in range(cap):
-            page_copy(s, r).start()
-        return carry
-
-    lax.fori_loop(0, n, start, 0)
+    )(hidden, w_proj, codes, *arrays)
+    flat = [o.reshape((n, o.shape[1] * o.shape[2]) + o.shape[3:]) for o in out[3:]]
+    return out[0], out[1], out[2], flat
+
+
+def layer_kernel(n, nm, *refs):
+    (ctx, hid, wo_in, wu_in, wd_in, wp_in, pages_in, where, lens, vec_out, back_out) = refs[:11]
+    (wo, wu, wd, wp, pages, load_sem, send_a, recv_a, mid_all, send_d, recv_d) = refs[11:22]
+    (seen, found, back, sem_s, sem_r, vec_s, vec_r, back_s, back_r) = refs[22:]
+    dp, mp = lax.axis_index("dp"), lax.axis_index("mp")
+    rows, width = hid.shape
+    cap, ptok = back.shape[1], pages.shape[1]
+    block = wo.shape[2]
+    step_cols = max(256, block)
+    per = step_cols // block
+    chunks = width // step_cols
+    loads = [
+        pltpu.make_async_copy(src, dst, load_sem.at[i])
+        for i, (src, dst) in enumerate(
+            ((wo_in, wo), (wu_in, wu), (wd_in, wd), (wp_in, wp), (pages_in, pages))
+        )
+    ]
+    for c in loads:
+        c.start()
+    barrier = pltpu.get_barrier_semaphore()
+    for k in range(1, n):
+        pl.semaphore_signal(
+            barrier, inc=1, device_id=((dp + k) % n, mp), device_id_type=MESH
+        )
+    for k in range(1, nm):
+        pl.semaphore_signal(
+            barrier, inc=1, device_id=(dp, (mp + k) % nm), device_id_type=MESH
+        )
+    pl.semaphore_wait(barrier, n - 1 + nm - 1)
+
+    def piece(w, j):
+        parts = [w[j * per + t] for t in range(per)]
+        return parts[0] if per == 1 else jnp.concatenate(parts, axis=1)
+
+    def mp_copy(stage, k, j, src, dst):
+        return pltpu.make_async_remote_copy(
+            src_ref=src,
+            dst_ref=dst,
+            send_sem=sem_s.at[stage, k - 1, j],
+            recv_sem=sem_r.at[stage, k - 1, j],
+            device_id=(dp, (mp + k) % nm),
+            device_id_type=MESH,
+        )
+
+    order = [k for k in range(1, nm) if k != 1] + [1]
+    started = []
+
+    loads[0].wait()
+    own = []
+    for j in range(chunks):
+        weight = piece(wo, j)
+        for k in order:
+            block_rows = ctx[pl.ds(pl.multiple_of((mp + k) % nm * rows, rows), rows), :]
+            send_a[k - 1, j] = add_rows(block_rows, weight).astype(jnp.bfloat16)
+            copy = mp_copy(0, k, j, send_a.at[k - 1, j], recv_a.at[k - 1, j])
+            copy.start()
+            started.append(copy)
+        own.append(add_rows(ctx[pl.ds(pl.multiple_of(mp * rows, rows), rows), :], weight))
+    sums = []
+    for j in range(chunks):
+        total = own[j]
+        for k in range(1, nm):
+            mp_copy(0, k, j, send_a.at[k - 1, j], recv_a.at[k - 1, j]).wait_recv()
+            total = total + recv_a[k - 1, j].astype(jnp.float32)
+        sums.append(total)
+    attn = jnp.concatenate(sums, axis=1)
+    mid = layer_norm(hid[...].astype(jnp.float32) + attn).astype(jnp.bfloat16)
+    mid_all[mp] = mid
+    for k in order:
+        copy = mp_copy(1, k, 0, mid_all.at[mp], mid_all.at[mp])
+        copy.start()
+        started.append(copy)
+    loads[1].wait()
+    loads[2].wait()
+    for k in range(1, nm):
+        mp_copy(1, k, 0, mid_all.at[mp], mid_all.at[mp]).wait_recv()
+    group_mid = mid_all[...].reshape(nm * rows, width)
+    inner = []
+    hidden_cols = wu.shape[1]
+    for j in range(hidden_cols // 256):
+        up = add_rows(group_mid, wu[:, j * 256 : (j + 1) * 256])
+        act = 0.5 * up * (1.0 + lax.erf(up * (0.5**0.5)))
+        inner.append(act.astype(jnp.bfloat16))
+    inner = jnp.concatenate(inner, axis=1)
+    for j in range(chunks):
+        down = add_rows(inner, piece(wd, j)).astype(jnp.bfloat16)
+        send_d[j] = down.reshape(nm, rows, step_cols)
+        for k in order:
+            copy = mp_copy(2, k, j, send_d.at[j, (mp + k) % nm], recv_d.at[k - 1, j])
+            copy.start()
+            started.append(copy)
+    sums = []
+    for j in range(chunks):
+        total = send_d[j, mp].astype(jnp.float32)
+        for k in range(1, nm):
+            mp_copy(2, k, j, send_d.at[j, mp], recv_d.at[k - 1, j]).wait_recv()
+            total = total + recv_d[k - 1, j].astype(jnp.float32)
+        sums.append(total)
+    mlp = jnp.concatenate(sums, axis=1)
+    state = layer_norm(mid_all[mp].astype(jnp.float32) + mlp).astype(jnp.bfloat16)
+    loads[3].wait()
+    proj = add_rows(state, wp[...])
+    norm = jnp.sqrt(jnp.sum(proj * proj, axis=-1, keepdims=True) + 1e-06)
+    vectors = (proj / norm).astype(jnp.bfloat16)
+    vec_out[...] = vectors
+    seen[dp] = vectors
+
+    def vec_copy(k):
+        return pltpu.make_async_remote_copy(
+            src_ref=seen.at[dp],
+            dst_ref=seen.at[dp],
+            send_sem=vec_s.at[k - 1],
+            recv_sem=vec_r.at[k - 1],
+            device_id=((dp + k) % n, mp),
+            device_id_type=MESH,
+        )
+
+    def back_copy(k):
+        return pltpu.make_async_remote_copy(
+            src_ref=found.at[k - 1],
+            dst_ref=back.at[dp],
+            send_sem=back_s.at[k - 1],
+            recv_sem=back_r.at[k - 1],
+            device_id=((dp - k + n) % n, mp),
+            device_id_type=MESH,
+        )
+
+    for k in range(1, n):
+        vec_copy(k).start()
+    loads[4].wait()
     token = lax.broadcasted_iota(jnp.int32, (ptok, rows), 0)
 
-    def work(s, carry):
-        pltpu.make_async_copy(buf.at[s], buf.at[s], sems.at[s]).wait()
-        vec = vec_ref[s]
-        for g in range(cap // group):
-            chunk = buf[s, pl.ds(g * group, group)].reshape(group * ptok, -1)
+    def match(source):
+        vec = seen[source]
+        best = []
+        for g in range(0, cap, 8):
+            slots = [where[source * cap + g + r] for r in range(8)]
+            chunk = jnp.concatenate([pages[slot] for slot in slots], axis=0)
             sim = lax.dot_general(
                 chunk, vec, (((1,), (1,)), ((), ())), preferred_element_type=jnp.float32
             )
-            best = []
-            for r in range(group):
-                length = lens_ref[where_ref[s * cap + g * group + r]]
+            for r in range(8):
                 part = sim[r * ptok : (r + 1) * ptok]
-                part = jnp.where(token < length, part, -1e30)
+                part = jnp.where(token < lens[slots[r]], part, -1e30)
                 best.append(jnp.max(part, axis=0, keepdims=True))
-            out_ref[s, pl.ds(g * group, group)] = jnp.concatenate(best, axis=0)
+        return jnp.concatenate(best, axis=0).astype(jnp.bfloat16)
+
+    back[dp] = match(dp)
+
+    def work(k, carry):
+        vec_copy(k).wait_recv()
+        found[k - 1] = match((dp - k + n) % n)
+        back_copy(k).start()
         return carry
 
-    lax.fori_loop(0, n, work, 0)
-
-
-def score_pages(where, lens, vecs, pages):
-    n, cap = where.shape
-    rows = vecs.shape[1]
-    grid_spec = pltpu.PrefetchScalarGridSpec(
-        num_scalar_prefetch=2,
-        grid=(1,),
-        in_specs=[
-            pl.BlockSpec(vecs.shape, lambda i, a, b: (0, 0, 0)),
-            pl.BlockSpec(memory_space=pl.ANY),
+    lax.fori_loop(1, n, work, 0)
+    for k in range(1, n):
+        back_copy(k).wait_recv()
+    back_out[...] = back[...]
+    for k in range(1, n):
+        vec_copy(k).wait_send()
+        back_copy(k).wait_send()
+    for c in started:
+        c.wait_send()
+
+
+def layer_and_score(n, nm, cap, ctx, hid, wo, wu, wd, wp, pages, where, lens):
+    rows, width = hid.shape
+    block = wo.shape[2]
+    step_cols = max(256, block)
+    chunks = width // step_cols
+    bf = jnp.bfloat16
+    vmem = pl.BlockSpec(memory_space=pltpu.VMEM)
+    smem = pl.BlockSpec(memory_space=pltpu.SMEM)
+    far = pl.BlockSpec(memory_space=pl.ANY)
+    dma = pltpu.SemaphoreType.DMA
+    scratch = [pltpu.VMEM(a.shape, a.dtype) for a in (wo, wu, wd, wp, pages)] + [
+        dma((5,)),
+        pltpu.VMEM((nm - 1, chunks, rows, step_cols), bf),
+        pltpu.VMEM((nm - 1, chunks, rows, step_cols), bf),
+        pltpu.VMEM((nm, rows, width), bf),
+        pltpu.VMEM((chunks, nm, rows, step_cols), bf),
+        pltpu.VMEM((nm - 1, chunks, rows, step_cols), bf),
+        pltpu.VMEM((n, rows, wp.shape[1]), bf),
+        pltpu.VMEM((n - 1, cap, rows), bf),
+        pltpu.VMEM((n, cap, rows), bf),
+        dma((3, nm - 1, chunks)),
+        dma((3, nm - 1, chunks)),
+        dma((n - 1,)),
+        dma((n - 1,)),
+        dma((n - 1,)),
+        dma((n - 1,)),
+    ]
+    return pl.pallas_call(
+        functools.partial(layer_kernel, n, nm),
+        out_shape=[
+            jax.ShapeDtypeStruct((rows, wp.shape[1]), bf),
+            jax.ShapeDtypeStruct((n, cap, rows), bf),
         ],
-        out_specs=pl.BlockSpec((n, cap, rows), lambda i, a, b: (0, 0, 0)),
-        scratch_shapes=[
-            pltpu.VMEM((n, cap) + pages.shape[1:], pages.dtype),
-            pltpu.SemaphoreType.DMA((n,)),
-        ],
-    )
-    return pl.pallas_call(
-        functools.partial(score_kernel, n, cap, rows),
-        grid_spec=grid_spec,
-        out_shape=jax.ShapeDtypeStruct((n, cap, rows), jnp.float32),
-        compiler_params=pltpu.CompilerParams(vmem_limit_bytes=40 * 2**20),
-    )(where.reshape(-1), lens, vecs, pages)
+        in_specs=[vmem, vmem, far, far, far, far, far, smem, smem],
+        out_specs=[vmem, vmem],
+        scratch_shapes=scratch,
+        compiler_params=pltpu.CompilerParams(
+            collective_id=1, has_side_effects=True, vmem_limit_bytes=40 * 2**20
+        ),
+    )(ctx, hid, wo, wu, wd, wp, pages, where, lens)
 
 
 def body(
@@ -238,23 +406,18 @@
     place = jnp.sum(earlier.astype(jnp.int32), axis=1)
     index = dest * cap + place
     codes = jnp.zeros((n * cap,), jnp.int32).at[index].set(slots % pg_dev)
-    where_local = lax.all_to_all(
-        codes.reshape(n, cap), "dp", split_axis=0, concat_axis=0, tiled=True
-    )
-
-    tokens, proj_w, (wq, wk, wv, rel, wo, wu, wd) = gather_all(
+    tokens, proj_w, where_local, (wq, wk, wv, rel, wo, wu, wd) = gather_all(
         n,
         nm,
         hidden.reshape(qry_dev * qlen, width),
         w_proj,
+        codes.reshape(n, 1, cap),
         (query_weight, w_key, w_value, rel_table, w_out, w_up, w_down),
     )
     group = nm * qry_dev
     flat = tokens.reshape(group * qlen, width)
     wq, wk, wv = (w.reshape(width, cols) for w in (wq, wk, wv))
     rel = rel.reshape(-1, width)
-    wo = jnp.transpose(wo, (1, 0, 2)).reshape(wo.shape[1], width)
-    wd = jnp.transpose(wd, (1, 0, 2)).reshape(wd.shape[1], width)
     wu = wu.reshape(width, -1)
     qsum = add_rows(flat, wq)
     ksum = add_rows(flat, wk)
@@ -280,29 +443,21 @@
     probs = jax.nn.softmax(logits, axis=-1).astype(jnp.bfloat16)
     context_rows = jnp.einsum("qhij,qjhd->qihd", probs, vx, preferred_element_type=jnp.float32)
     context_rows = context_rows.astype(jnp.bfloat16).reshape(group * qlen, cols)
-    attn_terms = add_rows(context_rows, wo)
-    attn = lax.psum_scatter(
-        attn_terms.astype(jnp.bfloat16), "mp", scatter_dimension=0, tiled=True
-    ).astype(jnp.float32)
-    own = hidden.reshape(qry_dev * qlen, width).astype(jnp.float32)
-    mid = layer_norm(own + attn).astype(jnp.bfloat16)
-    mid_all = lax.all_gather(mid, "mp", axis=0, tiled=True)
-    up = add_rows(mid_all, wu)
-    inner = jax.nn.gelu(up, approximate=False).astype(jnp.bfloat16)
-    down_terms = add_rows(inner, wd)
-    mlp = lax.psum_scatter(
-        down_terms.astype(jnp.bfloat16), "mp", scatter_dimension=0, tiled=True
-    ).astype(jnp.float32)
-    state = layer_norm(mid.astype(jnp.float32) + mlp).astype(jnp.bfloat16)
     width_out = w_proj.shape[1]
-    proj = add_rows(state, proj_w.reshape(width, width_out))
-    vectors = (proj / jnp.sqrt(jnp.sum(proj * proj, axis=-1, keepdims=True) + 1e-06)).astype(
-        jnp.bfloat16
+    vectors, back_home = layer_and_score(
+        n,
+        nm,
+        cap,
+        context_rows,
+        hidden.reshape(qry_dev * qlen, width),
+        wo,
+        wu,
+        wd,
+        proj_w.reshape(width, width_out),
+        pages,
+        where_local.reshape(-1),
+        page_len,
     )
-    spread = jnp.broadcast_to(vectors[None], (n,) + vectors.shape)
-    seen = lax.all_to_all(spread, "dp", split_axis=0, concat_axis=0, tiled=True)
-    best = score_pages(where_local, page_len, seen, pages).astype(jnp.bfloat16)
-    back_home = lax.all_to_all(best, "dp", split_axis=0, concat_axis=0, tiled=True)
     best = back_home.reshape(n * cap, qry_dev * qlen)[index].astype(jnp.float32)
     best = best.reshape(qry_dev, ncand, ppc, qry_dev, qlen)
     best = jnp.stack([best[q, :, :, q] for q in range(qry_dev)])

time: 220 us -> 152 us (0.69)
  waiting for transfers between devices: 44.9 us -> 0 us
  Pallas kernels: 95.9 us -> 120 us
  starting transfers between devices: 14.4 us -> 0 us
  between operations: 14.5 us -> 0.95 us
  matrix products: 19.9 us -> 12.7 us
  blocking collectives: 6.95 us -> 0 us
  other arithmetic: 7.2 us -> 3.76 us
    reduce_scatter x2 -> x0, waiting for transfers between devices: 32.1 us -> none  [the longest x1 18.7 us: body(): lax.psum_scatter(attn_terms.astype(jnp.bfloat16), 'mp', scatter_dimension...]
    pallas_call x1, Pallas kernels: 16.3 us -> 39.2 us  [layer_and_score(): pl.pallas_call(functools.partial(layer_kernel, n, nm), out_shape=[jax.Sha...]
    all_to_all x3 -> x0, starting transfers between devices: 14.3 us -> none  [the longest x1 5.51 us: body(): lax.all_to_all(codes.reshape(n, cap), 'dp', split_axis=0, concat_axis=0,...]
    all_to_all x3 -> x0, waiting for transfers between devices: 12.7 us -> none  [the longest x1 6.61 us: body(): lax.all_to_all(best, 'dp', split_axis=0, concat_axis=0, tiled=True)]
    dot_general x8 -> x5, matrix products: 13.3 us -> 4.45 us  [add_rows(): return jnp.dot(left, piece, preferred_element_type=jnp.float32)]
    all_gather x1 -> x0, blocking collectives: 6.95 us -> none  [body(): mid_all = lax.all_gather(mid, 'mp', axis=0, tiled=True)]
    reduce_sum x4 -> x0, other arithmetic: 4.31 us -> none  [the longest x2 2.22 us: layer_norm(): var = jnp.mean(centered * centered, axis=-1, keepdims=True)]
    reshape x3 -> x2, local copies, waits for them, and re-layouts: 2.96 us -> 0.75 us  [the longest x1 0.68 us: body(): codes.reshape(n, 1, cap)]
  transfers between devices with their start and end apart: 5 -> 0, of which waited for: 4 -> 0; matrix products, arithmetic and copies ran while one was open for 5% -> 0% of each run, Pallas kernels for 0% -> 0%
where the time goes in v2:
time: 152 us
  Pallas kernels  120 us (79%)
  local copies, waits for them, and re-layouts  13.9 us (9%)
  matrix products  12.7 us (8%)
  other arithmetic  3.76 us (2%)
    pallas_call x1, Pallas kernels, gather_all(): pl.pallas_call(functools.partial(gather_kernel, n, nm, count), out_shape=...  81.2 us
    pallas_call x1, Pallas kernels, layer_and_score(): pl.pallas_call(functools.partial(layer_kernel, n, nm), out_shape=[jax.Sha...  39.2 us
    unnamed x30, local copies, waits for them, and re-layouts  6.67 us
    dot_general x5, matrix products, add_rows(): return jnp.dot(left, piece, preferred_element_type=jnp.float32)  4.45 us

profile of v2, /device:TPU:0, one launch (start us, length us, event | category | flops | bytes accessed | tf_op | source)
XLA Modules:
  0.0 151.6 jit_solution(10764819091723288317)
XLA Ops:
  0.6 0.0 copy-start
  0.6 0.8 copy.34
  1.4 0.1 reshape.197
  1.6 1.1 gather_fusion
  2.7 0.2 convert_reduce_fusion
  2.9 1.0 scatter_custom_fusion
  3.9 0.7 reshape.198.refs_2_
  4.6 81.2 %shard_map.149 = (bf16[4,64,1024]{2,1,0:T(8,128)(2,1)}, bf16[8,4,32,128]{3,2,1,0:T(8,128)(2,1)}, s32[8,1,32]{2,1,0:T(1,128)}, bf16[8,2,64,256]{3,2,1,0:T(8,128)(...) custom-call(bf16[64,1024]{1,0:T(8,128)(2,1)} %bitcast.83, ...), custom_call_target="tpu_custom_call" | custom-call | tf_op jit(solution)/shard_map/pallas_call | solution.py:148
  85.8 1.6 %convolution_convert_fusion.5 = bf16[256,256]{1,0:T(8,128)(2,1)S(1)} fusion(bf16[256,1024]{1,0:T(8,128)(2,1)} %bitcast.88, bf16[1024,256]{1,0:T(8,128)(2,1)} %bitcast.97), kind=kOutput, calls=%fused_computation.21 | convolution fusion | flops 134283264 | bytes 1179648 | tf_op jit(solution)/shard_map/dot_general | solution.py:22
  87.5 0.5 broadcast.167
  88.0 1.3 reduce.3
  89.3 0.1 reshape.216.refs_7_
  89.4 0.9 reshape.207
  90.3 1.6 %convolution_convert_fusion.3 = bf16[256,256]{1,0:T(8,128)(2,1)S(1)} fusion(bf16[256,1024]{1,0:T(8,128)(2,1)} %bitcast.89, bf16[1024,256]{1,0:T(8,128)(2,1)} %bitcast.93), kind=kOutput, calls=%fused_computation.19 | convolution fusion | flops 134283264 | bytes 1179648 | tf_op jit(solution)/shard_map/dot_general | solution.py:22
  91.8 0.3 convolution_convert_fusion.4
  92.1 0.0 copy-done.9
  92.2 0.5 convolution_convert_fusion.1
  92.7 0.5 convolution_convert_fusion.2
  93.1 0.2 reshape.208
  93.3 0.2 reshape.209
  93.5 0.0 copy-start.13
  93.5 0.5 fusion.16
  94.0 0.3 copy-done.13
  94.2 1.4 fusion.1
  95.6 0.0 copy-done.12
  95.6 0.5 fusion.18
  96.1 1.4 fusion.3
  97.5 0.3 copy.38
  97.9 2.2 %fusion.11 = f32[8,4,32,32]{2,3,1,0:T(8,128)} fusion(f32[32,32,8,4]{0,1,3,2:T(8,128)S(1)} %copy.38, f32[32,32,8,4]{1,2,3,0:T(8,128)S(1)} %fusion.1, bf16[8,32,4,64]{3,2,1,0:T(4,128)(2,1)} %copy-done.12, bf16[8,32,4,64]{3,2,1,0:T(4,128)(2,1)S(1)} %reshape.208), kind=kOutput, calls=%fused_computation.14 | convolution fusion | flops 4292608 | bytes 655360 | tf_op jit(solution)/shard_map/qihd,qjhd->qhij/dot_general | solution.py:437
  100.1 0.0 copy-start.7
  100.1 1.5 %fusion.30 = f32[8,4,32]{2,1,0:T(4,128)S(1)} fusion(f32[8,4,32,32]{2,3,1,0:T(8,128)} %fusion.11), kind=kOutput, calls=%fused_computation.58 | output fusion | flops 65567 | bytes 135168 | tf_op jit(solution)/shard_map/sub | solution.py:443
  101.6 2.3 %fusion.12 = bf16[8,32,4,64]{3,1,2,0:T(8,128)(2,1)} fusion(bf16[8,32,4,64]{3,2,1,0:T(4,128)(2,1)} %reshape.207, f32[8,4,32]{2,1,0:T(4,128)S(1)} %fusion.30, f32[8,4,32,32]{2,3,1,0:T(8,128)} %fusion.11), kind=kOutput, calls=%fused_computation.18 | convolution fusion | flops 4359199 | bytes 397312 | tf_op jit(solution)/shard_map/qhij,qjhd->qihd/dot_general | solution.py:444
  103.9 1.1 copy.43
  105.0 0.2 reshape.212.refs_0_
  105.2 0.0 copy-done.2
  105.2 0.0 copy-done.4
  105.2 0.0 copy-done.5
  105.2 0.0 copy-done.6
  105.3 0.0 copy-start.1
  105.3 3.4 %copy-done.1 = bf16[256,128,128]{2,1,0:T(8,128)(2,1)S(1)} copy-done((bf16[256,128,128]{2,1,0:T(8,128)(2,1)S(1)}, bf16[256,128,128]{2,1,0:T(8,128)(2,1)}, u32[]{:S(2)}) %copy-start.1) | copy-done | bytes 8388632
  108.6 1.6 %copy-done.3 = bf16[8,2,512,128]{3,2,1,0:T(8,128)(2,1)S(1)} copy-done((bf16[8,2,512,128]{3,2,1,0:T(8,128)(2,1)S(1)}, bf16[8,2,512,128]{3,2,1,0:T(8,128)(2,1)}, u32[]{:S(2)}) %copy-start.3) | copy-done | bytes 2097176
  110.2 39.2 %shard_map.150 = (bf16[64,128]{1,0:T(8,128)(2,1)S(1)}, bf16[8,32,64]{2,1,0:T(8,128)(2,1)S(1)}) custom-call(bf16[256,256]{1,0:T(8,128)(2,1)S(1)} %reshape.212.refs_0_, bf16[64,1024]{1,0:T(8,128)(2,1)S(1)} %bitcast.84, bf16[8,256,128]{2,1,0:T(8,128)(2,1)S(1)} %bitcast.85, bf16[1024,1024]{1,0:T(8,128)(2,1)S(1)} %bitcast.80, bf16[8,1024,128]{2,1,0:T(8,128)(2,1)S(1)} %bitcast.81, ...), custom_call_target="tpu_custom_call" | custom-call | tf_op jit(solution)/shard_map/pallas_call | solution.py:362
  149.4 0.7 gather_fusion.1
  150.1 0.1 reshape.219
  150.2 0.1 fusion.29
  150.3 0.1 maximum_reduce_fusion
  150.4 0.7 reduce_sum.32
  151.0 0.6 copy.60
  (20 shorter events, 0.1 us)
Async XLA Ops:
  0.6 0.9 copy-start
  85.8 6.0 %copy-start.8 = (bf16[4,64,1024]{2,1,0:T(8,128)(2,1)S(1)}, bf16[4,64,1024]{2,1,0:T(8,128)(2,1)}, u32[]{:S(2)}) copy-start(bf16[4,64,1024]{2,1,0:T(8,128)(2,1)} %get-tuple-element.14) | copy-start | bytes 1572868
  85.8 6.0 %copy-start.11 = (bf16[8,2,64,256]{3,2,1,0:T(8,128)(2,1)S(1)}, bf16[8,2,64,256]{3,2,1,0:T(8,128)(2,1)}, u32[]{:S(2)}) copy-start(bf16[8,2,64,256]{3,2,1,0:T(8,128)(2,1)} %get-tuple-element.16) | copy-start | bytes 1572868
  85.8 6.4 %copy-start.9 = (bf16[8,2,32,1024]{3,2,1,0:T(8,128)(2,1)S(1)}, bf16[8,2,32,1024]{3,2,1,0:T(8,128)(2,1)}, u32[]{:S(2)}) copy-start(bf16[8,2,32,1024]{3,2,1,0:T(8,128)(2,1)} %get-tuple-element.18) | copy-start | bytes 3145732
  90.3 2.4 %copy-start.10 = (bf16[8,2,64,256]{3,2,1,0:T(8,128)(2,1)S(1)}, bf16[8,2,64,256]{3,2,1,0:T(8,128)(2,1)}, u32[]{:S(2)}) copy-start(bf16[8,2,64,256]{3,2,1,0:T(8,128)(2,1)} %get-tuple-element.17) | copy-start | bytes 1572868
  93.5 2.2 %copy-start.12 = (bf16[8,32,4,64]{3,2,1,0:T(4,128)(2,1)}, bf16[8,32,4,64]{3,2,1,0:T(4,128)(2,1)S(1)}, u32[]{:S(2)}) copy-start(bf16[8,32,4,64]{3,2,1,0:T(4,128)(2,1)S(1)} %reshape.209) | copy-start | bytes 393220
  93.5 0.7 copy-start.13
  100.0 5.2 %copy-start.2 = (bf16[8,2,64,1024]{3,2,1,0:T(8,128)(2,1)S(1)}, bf16[8,2,64,1024]{3,2,1,0:T(8,128)(2,1)}, u32[]{:S(2)}) copy-start(bf16[8,2,64,1024]{3,2,1,0:T(8,128)(2,1)} %get-tuple-element.20) | copy-start | bytes 6291460
  100.0 5.2 %copy-start.4 = (bf16[2,32,1024]{2,1,0:T(8,128)(2,1)S(1)}, bf16[2,32,1024]{2,1,0:T(8,128)(2,1)}, u32[]{:S(2)}) copy-start(bf16[2,32,1024]{2,1,0:T(8,128)(2,1)} %param.14) | copy-start | bytes 393220
  100.1 5.2 %copy-start.5 = (bf16[8,2,128,128]{3,2,1,0:T(8,128)(2,1)S(1)}, bf16[8,2,128,128]{3,2,1,0:T(8,128)(2,1)}, u32[]{:S(2)}) copy-start(bf16[8,2,128,128]{3,2,1,0:T(8,128)(2,1)} %get-tuple-element.19) | copy-start | bytes 1572868
  100.1 5.2 %copy-start.6 = (bf16[8,4,32,128]{3,2,1,0:T(8,128)(2,1)S(1)}, bf16[8,4,32,128]{3,2,1,0:T(8,128)(2,1)}, u32[]{:S(2)}) copy-start(bf16[8,4,32,128]{3,2,1,0:T(8,128)(2,1)} %get-tuple-element.22) | copy-start | bytes 786436
  100.1 5.2 %copy-start.7 = (s32[256]{0:T(256)S(1)}, s32[256]{0:T(256)}, u32[]{:S(2)}) copy-start(s32[256]{0:T(256)} %refs_8_.1) | copy-start | bytes 3076
  105.3 3.4 %copy-start.1 = (bf16[256,128,128]{2,1,0:T(8,128)(2,1)S(1)}, bf16[256,128,128]{2,1,0:T(8,128)(2,1)}, u32[]{:S(2)}) copy-start(bf16[256,128,128]{2,1,0:T(8,128)(2,1)} %refs_6_.1) | copy-start | bytes 25165828
  108.6 1.6 %copy-start.3 = (bf16[8,2,512,128]{3,2,1,0:T(8,128)(2,1)S(1)}, bf16[8,2,512,128]{3,2,1,0:T(8,128)(2,1)}, u32[]{:S(2)}) copy-start(bf16[8,2,512,128]{3,2,1,0:T(8,128)(2,1)} %get-tuple-element.21) | copy-start | bytes 6291460

commit v3 on v2

--- a/solution.py
+++ b/solution.py
@@ -23,17 +23,27 @@
 
 
 def gather_kernel(n, nm, count, *refs):
-    hid, wp, codes = refs[:3]
-    ins = refs[3 : 3 + count]
-    hid_out, wp_out, codes_out = refs[3 + count : 6 + count]
-    outs = refs[6 + count : 6 + 2 * count]
-    wp_own, local_sem, mp_send, mp_recv, code_send, code_recv, send_sem, recv_sem = refs[
-        6 + 2 * count :
-    ]
+    hid, wp, codes, rel = refs[:4]
+    ins = refs[4 : 4 + count]
+    hid_out, wp_out, codes_out, rel_out = refs[4 + count : 8 + count]
+    outs = refs[8 + count : 8 + 2 * count]
+    (
+        local_sem,
+        mp_send,
+        mp_recv,
+        code_send,
+        code_recv,
+        fwd_send,
+        fwd_recv,
+        send_sem,
+        recv_sem,
+    ) = refs[8 + 2 * count :]
     dp, mp = lax.axis_index("dp"), lax.axis_index("mp")
     half = n // 2
     row, col = dp // 2, dp % 2
     pos = row + col * (n - 1 - 2 * row)
+    part = rel.shape[2] // nm
+    share = pl.ds(pl.multiple_of(mp * part, part), part)
 
     def at(p):
         p = (p + 2 * n) % n
@@ -52,49 +62,20 @@
         )
     pl.semaphore_wait(barrier, n - 1 + nm - 1)
 
-    local = [pltpu.make_async_copy(wp, wp_own.at[mp], local_sem.at[0])]
-    local.append(pltpu.make_async_copy(hid, hid_out.at[mp], local_sem.at[1]))
-    for i in range(count):
-        local.append(pltpu.make_async_copy(ins[i], outs[i].at[dp], local_sem.at[2 + i]))
-    mp_copies = []
-    for which, (src, dst) in enumerate(((wp, wp_own), (hid, hid_out))):
-        for k in range(1, nm):
-            copy = pltpu.make_async_remote_copy(
-                src_ref=src,
-                dst_ref=dst.at[mp],
-                send_sem=mp_send.at[which, k - 1],
-                recv_sem=mp_recv.at[which, k - 1],
-                device_id=(dp, (mp + k) % nm),
-                device_id_type=MESH,
-            )
-            copy.start()
-            mp_copies.append(copy)
-
-    local.append(pltpu.make_async_copy(codes.at[dp], codes_out.at[dp], local_sem.at[2 + count]))
-    code_copies = []
-    for k in range(1, n):
-        copy = pltpu.make_async_remote_copy(
-            src_ref=codes.at[(dp + k) % n],
-            dst_ref=codes_out.at[dp],
-            send_sem=code_send.at[k - 1],
-            recv_sem=code_recv.at[k - 1],
-            device_id=((dp + k) % n, mp),
-            device_id_type=MESH,
-        )
-        copy.start()
-        code_copies.append(copy)
     pending = {}
+    forwards = []
 
     def send(step, i, way):
         owner = at(pos - step) if way == 0 else at(pos + step)
-        if i == count:
-            h = nm // 2
-            cut = pl.ds(way * h, h)
-            src = wp_own.at[cut] if step == 0 else wp_out.at[owner, cut]
-            dst = wp_out.at[owner, cut]
+        if i == 0:
+            dst = rel_out.at[owner, way, :, share]
+            src = rel.at[way, :, share] if step == 0 else dst
+        elif i == 1:
+            dst = wp_out.at[owner, mp, way]
+            src = wp.at[way] if step == 0 else dst
         else:
-            src = ins[i].at[way] if step == 0 else outs[i].at[owner, way]
-            dst = outs[i].at[owner, way]
+            dst = outs[i - 2].at[owner, way]
+            src = ins[i - 2].at[way] if step == 0 else dst
         copy = pltpu.make_async_remote_copy(
             src_ref=src,
             dst_ref=dst,
@@ -106,62 +87,115 @@
         copy.start()
         pending[step, i, way] = copy
 
+    def forward(step, i, way):
+        owner = at(pos - step) if way == 0 else at(pos + step)
+        piece = rel_out.at[owner, way, :, share] if i == 0 else wp_out.at[owner, mp, way]
+        for k in range(1, nm):
+            copy = pltpu.make_async_remote_copy(
+                src_ref=piece,
+                dst_ref=piece,
+                send_sem=fwd_send.at[step - 1, i, way, k - 1],
+                recv_sem=fwd_recv.at[step - 1, i, way, k - 1],
+                device_id=(dp, (mp + k) % nm),
+                device_id_type=MESH,
+            )
+            copy.start()
+            forwards.append(copy)
+
+    local = [
+        pltpu.make_async_copy(wp, wp_out.at[dp, mp], local_sem.at[0]),
+        pltpu.make_async_copy(hid, hid_out.at[mp], local_sem.at[1]),
+        pltpu.make_async_copy(codes.at[dp], codes_out.at[dp], local_sem.at[2]),
+        pltpu.make_async_copy(rel, rel_out.at[dp], local_sem.at[3]),
+    ]
+    for i in range(count):
+        local.append(pltpu.make_async_copy(ins[i], outs[i].at[dp], local_sem.at[4 + i]))
+    others = []
+
+    def start_others():
+        for which, (src, dst) in enumerate(((wp, wp_out.at[dp, mp]), (hid, hid_out.at[mp]))):
+            for k in range(1, nm):
+                others.append(
+                    pltpu.make_async_remote_copy(
+                        src_ref=src,
+                        dst_ref=dst,
+                        send_sem=mp_send.at[which, k - 1],
+                        recv_sem=mp_recv.at[which, k - 1],
+                        device_id=(dp, (mp + k) % nm),
+                        device_id_type=MESH,
+                    )
+                )
+        for k in range(1, n):
+            others.append(
+                pltpu.make_async_remote_copy(
+                    src_ref=codes.at[(dp + k) % n],
+                    dst_ref=codes_out.at[dp],
+                    send_sem=code_send.at[k - 1],
+                    recv_sem=code_recv.at[k - 1],
+                    device_id=((dp + k) % n, mp),
+                    device_id_type=MESH,
+                )
+            )
+        for c in others + local:
+            c.start()
+
     for step in range(n - 1):
-        for i in range(count + 1):
-            if step == 0 and i == count:
-                for c in local:
-                    c.start()
-                local[0].wait()
-                for c in mp_copies[: nm - 1]:
-                    c.wait_recv()
-                own = pltpu.make_async_copy(wp_own, wp_out.at[dp], local_sem.at[0])
-                own.start()
+        for i in range(count + 2):
             for way in range(2):
                 if step:
                     pending[step - 1, i, way].wait_recv()
                 send(step, i, way)
-    for (step, i, way), copy in pending.items():
-        if step == n - 2:
-            copy.wait_recv()
-    for c in mp_copies[nm - 1 :]:
-        c.wait_recv()
-    for c in code_copies:
+                if step and i < 2:
+                    forward(step, i, way)
+        if step == 0:
+            start_others()
+    for i in range(count + 2):
+        for way in range(2):
+            pending[n - 2, i, way].wait_recv()
+            if i < 2:
+                forward(n - 1, i, way)
+    for c in others:
         c.wait()
-    own.wait()
-    for c in local[1:]:
+    for c in local:
         c.wait()
-    for c in mp_copies:
-        c.wait_send()
+    for c in forwards:
+        c.wait()
     for copy in pending.values():
         copy.wait_send()
 
 
-def gather_all(n, nm, hidden, w_proj, codes, arrays):
-    arrays = [a.reshape((2, a.shape[0] // 2) + a.shape[1:]) for a in arrays]
+def gather_all(n, nm, hidden, w_proj, codes, rel, arrays):
+    def halves(a):
+        return a.reshape((2, a.shape[0] // 2) + a.shape[1:])
+
+    w_proj, rel = halves(w_proj), halves(rel)
+    arrays = [halves(a) for a in arrays]
     count = len(arrays)
     bf = jnp.bfloat16
+    dma = pltpu.SemaphoreType.DMA
     shapes = [
         jax.ShapeDtypeStruct((nm,) + hidden.shape, bf),
         jax.ShapeDtypeStruct((n, nm) + w_proj.shape, bf),
         jax.ShapeDtypeStruct(codes.shape, jnp.int32),
-    ] + [jax.ShapeDtypeStruct((n,) + a.shape, bf) for a in arrays]
+    ] + [jax.ShapeDtypeStruct((n,) + a.shape, bf) for a in [rel] + arrays]
     out = pl.pallas_call(
         functools.partial(gather_kernel, n, nm, count),
         out_shape=shapes,
-        in_specs=[pl.BlockSpec(memory_space=pl.ANY)] * (count + 3),
-        out_specs=[pl.BlockSpec(memory_space=pl.ANY)] * (count + 3),
+        in_specs=[pl.BlockSpec(memory_space=pl.ANY)] * (count + 4),
+        out_specs=[pl.BlockSpec(memory_space=pl.ANY)] * (count + 4),
         scratch_shapes=[
-            pltpu.VMEM((nm,) + w_proj.shape, bf),
-            pltpu.SemaphoreType.DMA((count + 3,)),
-            pltpu.SemaphoreType.DMA((2, nm - 1)),
-            pltpu.SemaphoreType.DMA((2, nm - 1)),
-            pltpu.SemaphoreType.DMA((n - 1,)),
-            pltpu.SemaphoreType.DMA((n - 1,)),
-            pltpu.SemaphoreType.DMA((n - 1, count + 1, 2)),
-            pltpu.SemaphoreType.DMA((n - 1, count + 1, 2)),
+            dma((count + 4,)),
+            dma((2, nm - 1)),
+            dma((2, nm - 1)),
+            dma((n - 1,)),
+            dma((n - 1,)),
+            dma((n - 1, 2, 2, nm - 1)),
+            dma((n - 1, 2, 2, nm - 1)),
+            dma((n - 1, count + 2, 2)),
+            dma((n - 1, count + 2, 2)),
         ],
         compiler_params=pltpu.CompilerParams(collective_id=0, has_side_effects=True),
-    )(hidden, w_proj, codes, *arrays)
+    )(hidden, w_proj, codes, rel, *arrays)
     flat = [o.reshape((n, o.shape[1] * o.shape[2]) + o.shape[3:]) for o in out[3:]]
     return out[0], out[1], out[2], flat
 
@@ -369,7 +403,7 @@
         out_specs=[vmem, vmem],
         scratch_shapes=scratch,
         compiler_params=pltpu.CompilerParams(
-            collective_id=1, has_side_effects=True, vmem_limit_bytes=40 * 2**20
+            collective_id=1, has_side_effects=True, vmem_limit_bytes=60 * 2**20
         ),
     )(ctx, hid, wo, wu, wd, wp, pages, where, lens)
 
@@ -406,13 +440,14 @@
     place = jnp.sum(earlier.astype(jnp.int32), axis=1)
     index = dest * cap + place
     codes = jnp.zeros((n * cap,), jnp.int32).at[index].set(slots % pg_dev)
-    tokens, proj_w, where_local, (wq, wk, wv, rel, wo, wu, wd) = gather_all(
+    tokens, proj_w, where_local, (rel, wq, wk, wv, wo, wu, wd) = gather_all(
         n,
         nm,
         hidden.reshape(qry_dev * qlen, width),
         w_proj,
         codes.reshape(n, 1, cap),
-        (query_weight, w_key, w_value, rel_table, w_out, w_up, w_down),
+        rel_table,
+        (query_weight, w_key, w_value, w_out, w_up, w_down),
     )
     group = nm * qry_dev
     flat = tokens.reshape(group * qlen, width)

time: 152 us -> 136 us (0.89)
  Pallas kernels: 120 us -> 113 us
  local copies, waits for them, and re-layouts: 13.9 us -> 9.93 us
  matrix products: 12.7 us -> 8.98 us
    pallas_call x1, Pallas kernels: 81.2 us -> 73.7 us  [gather_all(): pl.pallas_call(functools.partial(gather_kernel, n, nm, count), out_shape=...]
    unnamed x30 -> x14, local copies, waits for them, and re-layouts: 6.67 us -> 2.37 us
    dot_general x1, matrix products: 2.31 us -> 0.33 us  [body(): jnp.einsum('qhij,qjhd->qihd', probs, vx, preferred_element_type=jnp.float32)]
    dot_general x1, matrix products: 2.19 us -> 0.44 us  [body(): jnp.einsum('qihd,qjhd->qhij', qx, kx, preferred_element_type=jnp.float32)]
where the time goes in v3:
time: 136 us; the launch traced here: 135 us
  Pallas kernels  113 us (83%)
  local copies, waits for them, and re-layouts  9.93 us (7%)
  matrix products  8.98 us (7%)
  other arithmetic  2.42 us (2%)
    pallas_call x1, Pallas kernels, gather_all(): pl.pallas_call(functools.partial(gather_kernel, n, nm, count), out_shape=...  73.7 us
    pallas_call x1, Pallas kernels, layer_and_score(): pl.pallas_call(functools.partial(layer_kernel, n, nm), out_shape=[jax.Sha...  39.2 us
    dot_general x5, matrix products, add_rows(): return jnp.dot(left, piece, preferred_element_type=jnp.float32)  4.47 us

profile of v3, /device:TPU:0, one launch (start us, length us, event | category | flops | bytes accessed | tf_op | source)
XLA Modules:
  0.0 135.1 jit_solution(7125539618403991347)
XLA Ops:
  0.6 0.0 copy-start
  0.6 0.8 copy.34
  1.4 0.1 reshape.201
  1.6 0.0 copy-done
  1.6 1.1 gather_fusion
  2.7 0.2 convert_reduce_fusion
  2.9 1.0 scatter_custom_fusion
  3.9 0.7 reshape.202.refs_2_
  4.6 73.7 %shard_map.149 = (bf16[4,64,1024]{2,1,0:T(8,128)(2,1)}, bf16[8,4,2,16,128]{4,3,2,1,0:T(8,128)(2,1)}, s32[8,1,32]{2,1,0:T(1,128)}, bf16[8,2,32,1024]{3,2,1,0:T(8,...) custom-call(bf16[64,1024]{1,0:T(8,128)(2,1)} %bitcast.93, ...), custom_call_target="tpu_custom_call" | custom-call | tf_op jit(solution)/shard_map/pallas_call | solution.py:181
  78.3 0.0 copy-start.1
  78.4 0.0 copy-start.4
  78.4 0.0 copy-start.2
  78.4 1.6 %convolution_convert_fusion.5 = bf16[256,256]{1,0:T(8,128)(2,1)S(1)} fusion(bf16[256,1024]{1,0:T(8,128)(2,1)} %bitcast.81, bf16[1024,256]{1,0:T(8,128)(2,1)} %bitcast.96), kind=kOutput, calls=%fused_computation.21 | convolution fusion | flops 134283264 | bytes 1179648 | tf_op jit(solution)/shard_map/dot_general | solution.py:22
  80.0 0.5 broadcast.167
  80.5 1.3 reduce.3
  81.9 0.6 reshape.220.refs_7_
  82.5 0.2 reshape.211
  82.7 0.0 copy-start.3
  82.7 1.6 %convolution_convert_fusion.3 = bf16[256,256]{1,0:T(8,128)(2,1)S(1)} fusion(bf16[256,1024]{1,0:T(8,128)(2,1)} %bitcast.82, bf16[1024,256]{1,0:T(8,128)(2,1)} %bitcast.86), kind=kOutput, calls=%fused_computation.19 | convolution fusion | flops 134283264 | bytes 1179648 | tf_op jit(solution)/shard_map/dot_general | solution.py:22
  84.2 0.0 copy-done.1
  84.3 0.0 copy-done.4
  84.3 0.3 convolution_convert_fusion.4
  84.6 0.0 copy-done.2
  84.6 0.5 convolution_convert_fusion.1
  85.1 0.0 copy-done.3
  85.1 0.5 convolution_convert_fusion.2
  85.6 0.2 reshape.212
  85.7 0.2 reshape.213
  85.9 0.0 copy-start.5
  85.9 0.5 fusion.16
  86.4 0.2 copy-done.5
  86.6 1.4 %fusion.1 = f32[32,32,8,4]{1,2,3,0:T(8,128)S(1)} fusion(f32[4,512,8,32]{1,2,0,3:T(8,128)S(1)} %fusion.16, s32[32,32]{1,0:T(8,128)S(1)} %copy-done.5), kind=kOutput, calls=%fused_computation.4 | convolution fusion | flops 201850880 | bytes 2232320 | tf_op jit(solution)/shard_map/qhjb,jib->qhij/dot_general | solution.py:476
  88.0 0.5 fusion.18
  88.5 1.4 %fusion.3 = f32[32,32,8,4]{1,2,3,0:T(8,128)S(1)} fusion(f32[4,512,8,32]{1,2,0,3:T(8,128)S(1)} %fusion.18, s32[32,32]{1,0:T(8,128)S(1)} %copy-done.5), kind=kOutput, calls=%fused_computation.6 | convolution fusion | flops 201850880 | bytes 2232320 | tf_op jit(solution)/shard_map/qhib,ijb->qhij/dot_general | solution.py:474
  89.9 0.3 copy.38
  90.3 0.4 fusion.11
  90.7 0.2 fusion.30
  90.9 0.3 fusion.12
  91.2 0.1 copy.43
  91.4 0.9 reshape.216.refs_0_
  92.2 39.2 %shard_map.150 = (bf16[64,128]{1,0:T(8,128)(2,1)}, bf16[8,32,64]{2,1,0:T(8,128)(2,1)}) custom-call(bf16[256,256]{1,0:T(8,128)(2,1)} %reshape.216.refs_0_, bf16[64,1024]{1,0:T(8,128)(2,1)} %bitcast.94, bf16[8,256,128]{2,1,0:T(8,128)(2,1)} %bitcast.95, bf16[1024,1024]{1,0:T(8,128)(2,1)} %bitcast.90, bf16[8,1024,128]{2,1,0:T(8,128)(2,1)} %bitcast.91, ...), custom_call_target="tpu_custom_call" | custom-call | tf_op jit(solution)/shard_map/pallas_call | solution.py:396
  131.4 1.5 %gather_fusion.1 = bf16[128,64]{1,0:T(8,128)(2,1)S(1)} fusion(bf16[256,64]{1,0:T(8,128)(2,1)} %bitcast.92, s32[1024]{0:T(1024)S(1)} %pad_clamp_fusion), kind=kCustom, calls=%fused_computation.1 | custom fusion | bytes 33280 | tf_op jit(solution)/shard_map/gather | solution.py:496
  132.9 0.1 reshape.223
  133.0 0.1 fusion.29
  133.1 0.1 maximum_reduce_fusion
  133.1 0.7 reduce_sum.32
  133.8 1.3 copy.60
  (5 shorter events, 0.0 us)
Async XLA Ops:
  0.6 0.9 copy-start
  78.3 5.9 %copy-start.1 = (bf16[4,64,1024]{2,1,0:T(8,128)(2,1)S(1)}, bf16[4,64,1024]{2,1,0:T(8,128)(2,1)}, u32[]{:S(2)}) copy-start(bf16[4,64,1024]{2,1,0:T(8,128)(2,1)} %get-tuple-element.14) | copy-start | bytes 1572868
  78.4 5.9 %copy-start.4 = (bf16[8,2,64,256]{3,2,1,0:T(8,128)(2,1)S(1)}, bf16[8,2,64,256]{3,2,1,0:T(8,128)(2,1)}, u32[]{:S(2)}) copy-start(bf16[8,2,64,256]{3,2,1,0:T(8,128)(2,1)} %get-tuple-element.16) | copy-start | bytes 1572868
  78.4 6.2 %copy-start.2 = (bf16[8,2,32,1024]{3,2,1,0:T(8,128)(2,1)S(1)}, bf16[8,2,32,1024]{3,2,1,0:T(8,128)(2,1)}, u32[]{:S(2)}) copy-start(bf16[8,2,32,1024]{3,2,1,0:T(8,128)(2,1)} %get-tuple-element.18) | copy-start | bytes 3145732
  82.7 2.4 %copy-start.3 = (bf16[8,2,64,256]{3,2,1,0:T(8,128)(2,1)S(1)}, bf16[8,2,64,256]{3,2,1,0:T(8,128)(2,1)}, u32[]{:S(2)}) copy-start(bf16[8,2,64,256]{3,2,1,0:T(8,128)(2,1)} %get-tuple-element.17) | copy-start | bytes 1572868
  85.9 0.7 copy-start.5

commit v4 on v3

--- a/solution.py
+++ b/solution.py
@@ -203,7 +203,7 @@
 def layer_kernel(n, nm, *refs):
     (ctx, hid, wo_in, wu_in, wd_in, wp_in, pages_in, where, lens, vec_out, back_out) = refs[:11]
     (wo, wu, wd, wp, pages, load_sem, send_a, recv_a, mid_all, send_d, recv_d) = refs[11:22]
-    (seen, found, back, sem_s, sem_r, vec_s, vec_r, back_s, back_r) = refs[22:]
+    (seen, found, back, sem_s, sem_r, vec_s, vec_r, back_s, back_r, ring_s, ring_r) = refs[22:]
     dp, mp = lax.axis_index("dp"), lax.axis_index("mp")
     rows, width = hid.shape
     cap, ptok = back.shape[1], pages.shape[1]
@@ -214,7 +214,7 @@
     loads = [
         pltpu.make_async_copy(src, dst, load_sem.at[i])
         for i, (src, dst) in enumerate(
-            ((wo_in, wo), (wu_in, wu), (wd_in, wd), (wp_in, wp), (pages_in, pages))
+            ((wo_in, wo), (wu_in, wu), (wd_in, wd.at[dp]), (wp_in, wp), (pages_in, pages))
         )
     ]
     for c in loads:
@@ -230,8 +230,42 @@
         )
     pl.semaphore_wait(barrier, n - 1 + nm - 1)
 
+    half = n // 2
+    row, col = dp // 2, dp % 2
+    pos = row + col * (n - 1 - 2 * row)
+
+    def at(p):
+        p = (p + 2 * n) % n
+        h = p // half
+        return 2 * (p + h * (n - 1 - 2 * p)) + h
+
+    right, left = at(pos + 1), at(pos - 1)
+    ring = []
+
+    def advance(upto):
+        for step in range(len(ring), min(upto, n - 2) + 1):
+            copies = []
+            for way in range(2):
+                if step:
+                    ring[step - 1][way].wait_recv()
+                owner = at(pos - step) if way == 0 else at(pos + step)
+                dst = wd.at[owner, way]
+                copy = pltpu.make_async_remote_copy(
+                    src_ref=dst if step else wd_in.at[way],
+                    dst_ref=dst,
+                    send_sem=ring_s.at[step, way],
+                    recv_sem=ring_r.at[step, way],
+                    device_id=(right if way == 0 else left, mp),
+                    device_id_type=MESH,
+                )
+                copy.start()
+                copies.append(copy)
+            ring.append(copies)
+
+    advance(0)
+
     def piece(w, j):
-        parts = [w[j * per + t] for t in range(per)]
+        parts = [w[j * per + t].reshape(-1, block) for t in range(per)]
         return parts[0] if per == 1 else jnp.concatenate(parts, axis=1)
 
     def mp_copy(stage, k, j, src, dst):
@@ -258,6 +292,7 @@
             copy.start()
             started.append(copy)
         own.append(add_rows(ctx[pl.ds(pl.multiple_of(mp * rows, rows), rows), :], weight))
+    advance(1)
     sums = []
     for j in range(chunks):
         total = own[j]
@@ -265,6 +300,7 @@
             mp_copy(0, k, j, send_a.at[k - 1, j], recv_a.at[k - 1, j]).wait_recv()
             total = total + recv_a[k - 1, j].astype(jnp.float32)
         sums.append(total)
+    advance(2)
     attn = jnp.concatenate(sums, axis=1)
     mid = layer_norm(hid[...].astype(jnp.float32) + attn).astype(jnp.bfloat16)
     mid_all[mp] = mid
@@ -272,10 +308,12 @@
         copy = mp_copy(1, k, 0, mid_all.at[mp], mid_all.at[mp])
         copy.start()
         started.append(copy)
+    advance(3)
     loads[1].wait()
     loads[2].wait()
     for k in range(1, nm):
         mp_copy(1, k, 0, mid_all.at[mp], mid_all.at[mp]).wait_recv()
+    advance(4)
     group_mid = mid_all[...].reshape(nm * rows, width)
     inner = []
     hidden_cols = wu.shape[1]
@@ -283,6 +321,11 @@
         up = add_rows(group_mid, wu[:, j * 256 : (j + 1) * 256])
         act = 0.5 * up * (1.0 + lax.erf(up * (0.5**0.5)))
         inner.append(act.astype(jnp.bfloat16))
+        if j % 2 == 0:
+            advance(5 + j // 2)
+    advance(n - 2)
+    for copy in ring[n - 2]:
+        copy.wait_recv()
     inner = jnp.concatenate(inner, axis=1)
     for j in range(chunks):
         down = add_rows(inner, piece(wd, j)).astype(jnp.bfloat16)
@@ -364,6 +407,9 @@
         back_copy(k).wait_send()
     for c in started:
         c.wait_send()
+    for copies in ring:
+        for c in copies:
+            c.wait_send()
 
 
 def layer_and_score(n, nm, cap, ctx, hid, wo, wu, wd, wp, pages, where, lens):
@@ -376,7 +422,9 @@
     smem = pl.BlockSpec(memory_space=pltpu.SMEM)
     far = pl.BlockSpec(memory_space=pl.ANY)
     dma = pltpu.SemaphoreType.DMA
-    scratch = [pltpu.VMEM(a.shape, a.dtype) for a in (wo, wu, wd, wp, pages)] + [
+    wd = wd.reshape((2, wd.shape[0] // 2) + wd.shape[1:])
+    shapes = [wo.shape, wu.shape, (n,) + wd.shape, wp.shape, pages.shape]
+    scratch = [pltpu.VMEM(shape, bf) for shape in shapes] + [
         dma((5,)),
         pltpu.VMEM((nm - 1, chunks, rows, step_cols), bf),
         pltpu.VMEM((nm - 1, chunks, rows, step_cols), bf),
@@ -392,6 +440,8 @@
         dma((n - 1,)),
         dma((n - 1,)),
         dma((n - 1,)),
+        dma((n - 1, 2)),
+        dma((n - 1, 2)),
     ]
     return pl.pallas_call(
         functools.partial(layer_kernel, n, nm),
@@ -440,14 +490,14 @@
     place = jnp.sum(earlier.astype(jnp.int32), axis=1)
     index = dest * cap + place
     codes = jnp.zeros((n * cap,), jnp.int32).at[index].set(slots % pg_dev)
-    tokens, proj_w, where_local, (rel, wq, wk, wv, wo, wu, wd) = gather_all(
+    tokens, proj_w, where_local, (rel, wq, wk, wv, wo, wu) = gather_all(
         n,
         nm,
         hidden.reshape(qry_dev * qlen, width),
         w_proj,
         codes.reshape(n, 1, cap),
         rel_table,
-        (query_weight, w_key, w_value, w_out, w_up, w_down),
+        (query_weight, w_key, w_value, w_out, w_up),
     )
     group = nm * qry_dev
     flat = tokens.reshape(group * qlen, width)
@@ -487,7 +537,7 @@
         hidden.reshape(qry_dev * qlen, width),
         wo,
         wu,
-        wd,
+        w_down,
         proj_w.reshape(width, width_out),
         pages,
         where_local.reshape(-1),

time: 136 us -> 131 us (0.963)
  Pallas kernels: 113 us -> 109 us
    pallas_call x1, Pallas kernels: 73.7 us -> 53.8 us  [gather_all(): pl.pallas_call(functools.partial(gather_kernel, n, nm, count), out_shape=...]
    pallas_call x1, Pallas kernels: 39.2 us -> 54.9 us  [layer_and_score(): pl.pallas_call(functools.partial(layer_kernel, n, nm), out_shape=[jax.Sha...]
where the time goes in v4:
time: 131 us
  Pallas kernels  109 us (83%)
  local copies, waits for them, and re-layouts  9.93 us (8%)
  matrix products  9 us (7%)
  other arithmetic  2.42 us (2%)
    pallas_call x1, Pallas kernels, layer_and_score(): pl.pallas_call(functools.partial(layer_kernel, n, nm), out_shape=[jax.Sha...  54.9 us
    pallas_call x1, Pallas kernels, gather_all(): pl.pallas_call(functools.partial(gather_kernel, n, nm, count), out_shape=...  53.8 us
    dot_general x5, matrix products, add_rows(): return jnp.dot(left, piece, preferred_element_type=jnp.float32)  4.47 us

profile of v4, /device:TPU:0, one launch (start us, length us, event | category | flops | bytes accessed | tf_op | source)
XLA Modules:
  0.0 131.0 jit_solution(15378478583205938128)
XLA Ops:
  0.6 0.0 copy-start
  0.6 0.8 copy.34
  1.4 0.1 reshape.198
  1.6 0.0 copy-done
  1.6 1.1 gather_fusion
  2.7 0.2 convert_reduce_fusion
  2.9 1.0 scatter_custom_fusion
  3.9 0.7 reshape.199.refs_2_
  4.6 53.8 %shard_map.149 = (bf16[4,64,1024]{2,1,0:T(8,128)(2,1)}, bf16[8,4,2,16,128]{4,3,2,1,0:T(8,128)(2,1)}, s32[8,1,32]{2,1,0:T(1,128)}, bf16[8,2,32,1024]{3,2,1,0:T(8,...) custom-call(bf16[64,1024]{1,0:T(8,128)(2,1)} %bitcast.91, ...), custom_call_target="tpu_custom_call" | custom-call | tf_op jit(solution)/shard_map/pallas_call | solution.py:181
  58.4 0.0 copy-start.1
  58.4 0.0 copy-start.4
  58.4 0.0 copy-start.2
  58.4 1.6 %convolution_convert_fusion.5 = bf16[256,256]{1,0:T(8,128)(2,1)S(1)} fusion(bf16[256,1024]{1,0:T(8,128)(2,1)} %bitcast.80, bf16[1024,256]{1,0:T(8,128)(2,1)} %bitcast.94), kind=kOutput, calls=%fused_computation.21 | convolution fusion | flops 134283264 | bytes 1179648 | tf_op jit(solution)/shard_map/dot_general | solution.py:22
  60.1 0.5 broadcast.167
  60.6 1.3 %reduce.3 = s32[8,32]{1,0:T(8,128)S(1)} reduce(s32[8,1,32]{2,1,0:T(1,128)} %get-tuple-element.21, s32[]{:T(128)} %broadcast.167), dimensions={1}, to_apply=%get-tuple-element.21.reduce_sub_computation.3 | reduce | bytes 2052 | tf_op jit(solution)/shard_map/pallas_call | solution.py:181
  61.9 0.6 reshape.216.refs_7_
  62.6 0.2 reshape.207
  62.7 0.0 copy-start.3
  62.7 1.6 %convolution_convert_fusion.3 = bf16[256,256]{1,0:T(8,128)(2,1)S(1)} fusion(bf16[256,1024]{1,0:T(8,128)(2,1)} %bitcast.81, bf16[1024,256]{1,0:T(8,128)(2,1)} %bitcast.86), kind=kOutput, calls=%fused_computation.19 | convolution fusion | flops 134283264 | bytes 1179648 | tf_op jit(solution)/shard_map/dot_general | solution.py:22
  64.3 0.0 copy-done.1
  64.3 0.0 copy-done.4
  64.3 0.3 convolution_convert_fusion.4
  64.6 0.0 copy-done.2
  64.6 0.5 convolution_convert_fusion.1
  65.1 0.0 copy-done.3
  65.1 0.5 convolution_convert_fusion.2
  65.6 0.2 reshape.208
  65.8 0.2 reshape.209
  66.0 0.0 copy-start.5
  66.0 0.5 fusion.16
  66.5 0.2 copy-done.5
  66.7 1.4 %fusion.1 = f32[32,32,8,4]{1,2,3,0:T(8,128)S(1)} fusion(f32[4,512,8,32]{1,2,0,3:T(8,128)S(1)} %fusion.16, s32[32,32]{1,0:T(8,128)S(1)} %copy-done.5), kind=kOutput, calls=%fused_computation.4 | convolution fusion | flops 201850880 | bytes 2232320 | tf_op jit(solution)/shard_map/qhjb,jib->qhij/dot_general | solution.py:526
  68.1 0.5 fusion.18
  68.6 1.4 %fusion.3 = f32[32,32,8,4]{1,2,3,0:T(8,128)S(1)} fusion(f32[4,512,8,32]{1,2,0,3:T(8,128)S(1)} %fusion.18, s32[32,32]{1,0:T(8,128)S(1)} %copy-done.5), kind=kOutput, calls=%fused_computation.6 | convolution fusion | flops 201850880 | bytes 2232320 | tf_op jit(solution)/shard_map/qhib,ijb->qhij/dot_general | solution.py:524
  70.0 0.3 copy.38
  70.3 0.4 fusion.11
  70.8 0.2 fusion.30
  71.0 0.3 fusion.12
  71.3 0.1 copy.43
  71.4 0.9 reshape.212.refs_0_
  72.3 54.9 %shard_map.150 = (bf16[64,128]{1,0:T(8,128)(2,1)}, bf16[8,32,64]{2,1,0:T(8,128)(2,1)}) custom-call(bf16[256,256]{1,0:T(8,128)(2,1)} %reshape.212.refs_0_, bf16[64,1024]{1,0:T(8,128)(2,1)} %bitcast.92, bf16[8,256,128]{2,1,0:T(8,128)(2,1)} %bitcast.93, bf16[1024,1024]{1,0:T(8,128)(2,1)} %bitcast.85, bf16[2,512,128]{2,1,0:T(8,128)(2,1)} %bitcast.96, ...), custom_call_target="tpu_custom_call" | custom-call | tf_op jit(solution)/shard_map/pallas_call | solution.py:446
  127.2 1.5 %gather_fusion.1 = bf16[128,64]{1,0:T(8,128)(2,1)S(1)} fusion(bf16[256,64]{1,0:T(8,128)(2,1)} %bitcast.90, s32[1024]{0:T(1024)S(1)} %pad_clamp_fusion), kind=kCustom, calls=%fused_computation.1 | custom fusion | bytes 33280 | tf_op jit(solution)/shard_map/gather | solution.py:546
  128.7 0.1 reshape.219
  128.9 0.1 fusion.29
  128.9 0.1 maximum_reduce_fusion
  129.0 0.7 reduce_sum.32
  129.7 1.3 %copy.60 = bf16[2,32,128]{2,1,0:T(8,128)(2,1)} copy(bf16[2,32,128]{2,1,0:T(8,128)(2,1)} %bitcast.107) | data formatting | bytes 32768
  (5 shorter events, 0.0 us)
Async XLA Ops:
  0.6 0.9 copy-start
  58.4 5.9 %copy-start.1 = (bf16[4,64,1024]{2,1,0:T(8,128)(2,1)S(1)}, bf16[4,64,1024]{2,1,0:T(8,128)(2,1)}, u32[]{:S(2)}) copy-start(bf16[4,64,1024]{2,1,0:T(8,128)(2,1)} %get-tuple-element.13) | copy-start | bytes 1572868
  58.4 5.9 %copy-start.4 = (bf16[8,2,64,256]{3,2,1,0:T(8,128)(2,1)S(1)}, bf16[8,2,64,256]{3,2,1,0:T(8,128)(2,1)}, u32[]{:S(2)}) copy-start(bf16[8,2,64,256]{3,2,1,0:T(8,128)(2,1)} %get-tuple-element.15) | copy-start | bytes 1572868
  58.4 6.2 %copy-start.2 = (bf16[8,2,32,1024]{3,2,1,0:T(8,128)(2,1)S(1)}, bf16[8,2,32,1024]{3,2,1,0:T(8,128)(2,1)}, u32[]{:S(2)}) copy-start(bf16[8,2,32,1024]{3,2,1,0:T(8,128)(2,1)} %get-tuple-element.17) | copy-start | bytes 3145732
  62.7 2.4 %copy-start.3 = (bf16[8,2,64,256]{3,2,1,0:T(8,128)(2,1)S(1)}, bf16[8,2,64,256]{3,2,1,0:T(8,128)(2,1)}, u32[]{:S(2)}) copy-start(bf16[8,2,64,256]{3,2,1,0:T(8,128)(2,1)} %get-tuple-element.16) | copy-start | bytes 1572868
  66.0 0.7 copy-start.5
